TPU v7x, 32 devices: a whole 2x2x4 slice. The times are simulated.
32 devices in a mesh: seq: 8 (over z, x), head: 4 (over y, core).
Axes of the slice: x: 2, y: 2, z: 4, core: 2. Of those that a mesh axis runs over, the one named last changes fastest.
Arguments:
- queries: bfloat16 [2048, 32, 128], P('seq', 'head')
- keys: bfloat16 [2048, 4, 128], P('seq', 'head')
- block_order: int32 [32], P('seq'), may hold values from 0 to 31, each once
- gate_query: bfloat16 [4, 128, 128], P('head'), may hold values from -0.5 to 0.5
- gate_key: bfloat16 [4, 384, 128], P('head'), may hold values from -0.3125 to 0.3125
Outputs:
- loss: float32 [], replicated
- grad_query: float32 [4, 128, 128], P('head')
- grad_key: float32 [4, 384, 128], P('head')
Inputs may be any that keep to these rules, and one draw needn't show every extreme that they name: `block_order`: each block position appears exactly once.
All inputs are finite; a program needn't handle non-finite values.
Results may differ from a plain program's by a relative error of at most 0.0029.
Values may be sent and summed in bfloat16 or wider, within the bound.
A program may use at most 64 MiB of HBM per device.

v0:
```python
import math

import jax
import jax.numpy as jnp
from jax import lax
from jax.sharding import PartitionSpec as P

BLOCK = 64


HIGH = lax.Precision.HIGHEST


def passed_along(block, axis, distance):
    devices = range(lax.axis_size(axis))
    route = [((i - distance) % len(devices), i) for i in devices]
    return lax.ppermute(block, axis, route)


def shards(queries, keys, block_order, gate_query, gate_key):
    tok, group, width = queries.shape
    local_blocks = tok // BLOCK
    seq_count = lax.axis_size("seq")
    all_blocks = local_blocks * seq_count
    rows = group * tok
    scale = width ** (-0.5)
    key_blocks = keys[:, 0, :].reshape(local_blocks, BLOCK, width)
    qmat = queries.transpose(1, 0, 2).reshape(rows, width)
    offsets = jnp.arange(BLOCK, dtype=jnp.int32)
    qpos_tok = (block_order[:, None] * BLOCK + offsets[None, :]).reshape(tok)
    qpos = jnp.tile(qpos_tok, group)
    qlast = jnp.max(qpos_tok)

    def fold(carry, piece, start):
        keyp, posp = piece
        count = keyp.shape[0]
        span = math.gcd(count, 8)

        def one(step, inner):
            kblk = keyp.reshape(span * BLOCK, width)
            kpos = (posp[:, None] * BLOCK + offsets[None, :]).reshape(span * BLOCK)

            def work(state):
                blockmax, rmax, rsum = state
                scores = (
                    lax.dot_general(
                        qmat, kblk, (((1,), (1,)), ((), ())), preferred_element_type=jnp.float32
                    )
                    * scale
                )
                scores = jnp.where(kpos[None, :] > qpos[:, None], -1e30, scores)
                bmax = jnp.max(scores.reshape(rows, span, BLOCK), axis=-1)
                column = start + step * span
                blockmax = lax.dynamic_update_slice(blockmax, bmax, (jnp.int32(0), column))
                newmax = jnp.maximum(rmax, jnp.max(scores, axis=-1))
                rsum = rsum * jnp.exp(rmax - newmax) + jnp.sum(
                    jnp.exp(scores - newmax[:, None]), axis=-1
                )
                return (blockmax, newmax, rsum)

            return lax.cond(jnp.min(posp) * BLOCK > qlast, lambda state: state, work, inner)

        return lax.fori_loop(0, count // span, one, carry)

    init = (
        jnp.full((rows, all_blocks), -1e30, jnp.float32),
        jnp.full((rows,), -1e30, jnp.float32),
        jnp.zeros((rows,), jnp.float32),
    )

    def turn(step, state):
        carry, kcur, pcur = state
        source = (lax.axis_index("seq") - step) % seq_count
        carry = fold(carry, (kcur, pcur), source * local_blocks)
        kcur, pcur = passed_along((kcur, pcur), "seq", 1)
        return (carry, kcur, pcur)

    carry, kcur, pcur = lax.fori_loop(0, seq_count - 1, turn, (init, key_blocks, block_order))
    source = (lax.axis_index("seq") - (seq_count - 1)) % seq_count
    carry = fold(carry, (kcur, pcur), source * local_blocks)
    blockmax, rmax, rsum = carry
    lse = rmax + jnp.log(rsum)
    probs = jnp.exp(blockmax - lse[:, None])
    pooled = jnp.max(probs.reshape(group, local_blocks, BLOCK, all_blocks), axis=2)
    target = pooled / jnp.sum(pooled, axis=-1, keepdims=True)
    qpool = jnp.mean(
        queries.reshape(local_blocks, BLOCK, group, width), axis=1, dtype=jnp.float32
    ).astype(jnp.bfloat16)
    kmean = jnp.mean(key_blocks, axis=1, dtype=jnp.float32).astype(jnp.bfloat16)
    kpool = jnp.concatenate(
        [jnp.max(key_blocks, axis=1), jnp.min(key_blocks, axis=1), kmean], axis=-1
    )
    qproj = jnp.einsum("bgd,de->gbe", qpool, gate_query[0], preferred_element_type=jnp.float32)
    kproj_own = jnp.dot(kpool, gate_key[0], preferred_element_type=jnp.float32)
    kproj, all_order = (
        lax.all_gather(kproj_own, "seq", axis=0, tiled=True),
        lax.all_gather(block_order, "seq", axis=0, tiled=True),
    )
    gscale = gate_query.shape[2] ** (-0.5)
    logits = jnp.einsum("gbe,ce->gbc", qproj, kproj, precision=HIGH) * gscale
    logits = jnp.where(all_order[None, None, :] > block_order[None, :, None], -1e30, logits)
    logp = jax.nn.log_softmax(logits, axis=-1)
    total = group * keys.shape[1] * lax.axis_size("head") * all_blocks
    safe = jnp.log(jnp.where(target > 0, target, 1.0))
    loss_part = jnp.sum(jnp.where(target > 0, target * (safe - logp), 0.0)) / total
    rowtot = jnp.sum(target, axis=-1, keepdims=True)
    dlogit = (jnp.exp(logp) * rowtot - target) / total
    dqproj = jnp.einsum("gbc,ce->gbe", dlogit, kproj, precision=HIGH) * gscale
    dkproj = jnp.einsum("gbc,gbe->ce", dlogit, qproj, precision=HIGH) * gscale
    grad_q = jnp.einsum("bgd,gbe->de", qpool.astype(jnp.float32), dqproj, precision=HIGH)
    dk_own = lax.psum_scatter(dkproj, "seq", scatter_dimension=0, tiled=True)
    grad_k = jnp.dot(kpool.astype(jnp.float32).T, dk_own, precision=HIGH)
    grad_q, grad_k = lax.psum((grad_q, grad_k), "seq")
    loss = lax.psum(loss_part, ("seq", "head"))
    return (loss, grad_q[None], grad_k[None])


def solution(mesh):
    return jax.shard_map(
        shards,
        mesh=mesh,
        in_specs=(
            P("seq", "head", None),
            P("seq", "head", None),
            P("seq"),
            P("head", None, None),
            P("head", None, None),
        ),
        out_specs=(P(), P("head", None, None), P("head", None, None)),
        check_vma=False,
    )
```

profile of v0, /device:TPU:0, one launch (start us, length us, event | category | flops | bytes accessed | tf_op | source)
XLA Modules:
  0.0 238.1 jit_solution(8332151913764015418)
XLA Ops:
  11.9 66.8 %while.46 = (s32[]{:T(128)}, f32[2048,32]{0,1:T(8,128)S(1)}, f32[2048]{0:T(1024)S(1)}, f32[2048]{0:T(1024)S(1)}, bf16[4,64,128]{2,1,0:T(8,128)(2,1)S(1)}, /*inde...) while((s32[]{:T(128)}, f32[2048,32]{0,1:T(8,128)S(1)}, ...), condition=%wide.region_8.9_spmd.clone, body=%wide.region_1.8_spmd.clone.sunk | while | flops 137883920 | bytes 7518438 | solution.py:78
  12.5 2.9 %collective-permute-start = (bf16[4,64,128]{2,1,0:T(8,128)(2,1)}, bf16[4,64,128]{2,1,0:T(8,128)(2,1)S(1)}, u32[]{:S(2)}, u32[]{:S(2)}) collective-permute-start(bf16[4,64,128]{2,1,0:T(8,128)(2,1)} %copy.52), channel_id=1, source_target_pairs={{28,0},{0,4},{4,8},{8,12},{12,16},{16,20},{20,24},{24,28},{29,1},{... | collective-permute-start | bytes 196616 | tf_op jit(solution)/shard_map/while/body/eval_jaxpr/ppermute | solution.py:17
  16.0 1.5 collective-permute-start.1
  20.1 2.7 %conditional.5 = (f32[2048,32]{0,1:T(8,128)S(1)}, f32[2048]{0:T(1024)S(1)}, f32[2048]{0:T(1024)S(1)}) conditional(s32[]{:T(128)} %convert_element_type.50, (s32[4]{0:T(128)}, s32[64]{0:T(128)S(1)}, s32[256]{0:T(256)S(1)}, bf16[4,64,128]{2,1,0:T(8,128)(2,1)}, bf16[2048,128]{1,0:T(8,128)(2,1)S(1)}, /*index=5*/s32[]{:T(128)}, s32[]{:T(128)}, ...), branch_computations={%region_3.6_spmd, %region_7.7_spmd} | conditional | flops 137883904 | bytes 7108087 | solution.py:61
  25.5 1.5 collective-permute-start.1
  29.7 2.7 %conditional.5 = (f32[2048,32]{0,1:T(8,128)S(1)}, f32[2048]{0:T(1024)S(1)}, f32[2048]{0:T(1024)S(1)}) conditional(s32[]{:T(128)} %convert_element_type.50, (s32[4]{0:T(128)}, s32[64]{0:T(128)S(1)}, s32[256]{0:T(256)S(1)}, bf16[4,64,128]{2,1,0:T(8,128)(2,1)}, bf16[2048,128]{1,0:T(8,128)(2,1)S(1)}, /*index=5*/s32[]{:T(128)}, s32[]{:T(128)}, ...), branch_computations={%region_3.6_spmd, %region_7.7_spmd} | conditional | flops 137883904 | bytes 7108087 | solution.py:61
  33.0 1.5 collective-permute-start
  35.0 1.5 collective-permute-start.1
  39.2 2.7 %conditional.5 = (f32[2048,32]{0,1:T(8,128)S(1)}, f32[2048]{0:T(1024)S(1)}, f32[2048]{0:T(1024)S(1)}) conditional(s32[]{:T(128)} %convert_element_type.50, (s32[4]{0:T(128)}, s32[64]{0:T(128)S(1)}, s32[256]{0:T(256)S(1)}, bf16[4,64,128]{2,1,0:T(8,128)(2,1)}, bf16[2048,128]{1,0:T(8,128)(2,1)S(1)}, /*index=5*/s32[]{:T(128)}, s32[]{:T(128)}, ...), branch_computations={%region_3.6_spmd, %region_7.7_spmd} | conditional | flops 137883904 | bytes 7108087 | solution.py:61
  47.2 2.7 %conditional.5 = (f32[2048,32]{0,1:T(8,128)S(1)}, f32[2048]{0:T(1024)S(1)}, f32[2048]{0:T(1024)S(1)}) conditional(s32[]{:T(128)} %convert_element_type.50, (s32[4]{0:T(128)}, s32[64]{0:T(128)S(1)}, s32[256]{0:T(256)S(1)}, bf16[4,64,128]{2,1,0:T(8,128)(2,1)}, bf16[2048,128]{1,0:T(8,128)(2,1)S(1)}, /*index=5*/s32[]{:T(128)}, s32[]{:T(128)}, ...), branch_computations={%region_3.6_spmd, %region_7.7_spmd} | conditional | flops 137883904 | bytes 7108087 | solution.py:61
  52.7 1.5 collective-permute-start.1
  56.9 2.7 %conditional.5 = (f32[2048,32]{0,1:T(8,128)S(1)}, f32[2048]{0:T(1024)S(1)}, f32[2048]{0:T(1024)S(1)}) conditional(s32[]{:T(128)} %convert_element_type.50, (s32[4]{0:T(128)}, s32[64]{0:T(128)S(1)}, s32[256]{0:T(256)S(1)}, bf16[4,64,128]{2,1,0:T(8,128)(2,1)}, bf16[2048,128]{1,0:T(8,128)(2,1)S(1)}, /*index=5*/s32[]{:T(128)}, s32[]{:T(128)}, ...), branch_computations={%region_3.6_spmd, %region_7.7_spmd} | conditional | flops 137883904 | bytes 7108087 | solution.py:61
  60.2 1.5 collective-permute-start
  62.2 1.5 collective-permute-start.1
  66.4 2.7 %conditional.5 = (f32[2048,32]{0,1:T(8,128)S(1)}, f32[2048]{0:T(1024)S(1)}, f32[2048]{0:T(1024)S(1)}) conditional(s32[]{:T(128)} %convert_element_type.50, (s32[4]{0:T(128)}, s32[64]{0:T(128)S(1)}, s32[256]{0:T(256)S(1)}, bf16[4,64,128]{2,1,0:T(8,128)(2,1)}, bf16[2048,128]{1,0:T(8,128)(2,1)S(1)}, /*index=5*/s32[]{:T(128)}, s32[]{:T(128)}, ...), branch_computations={%region_3.6_spmd, %region_7.7_spmd} | conditional | flops 137883904 | bytes 7108087 | solution.py:61
  69.8 1.5 collective-permute-start
  71.8 1.5 collective-permute-start.1
  75.9 2.7 %conditional.5 = (f32[2048,32]{0,1:T(8,128)S(1)}, f32[2048]{0:T(1024)S(1)}, f32[2048]{0:T(1024)S(1)}) conditional(s32[]{:T(128)} %convert_element_type.50, (s32[4]{0:T(128)}, s32[64]{0:T(128)S(1)}, s32[256]{0:T(256)S(1)}, bf16[4,64,128]{2,1,0:T(8,128)(2,1)}, bf16[2048,128]{1,0:T(8,128)(2,1)S(1)}, /*index=5*/s32[]{:T(128)}, s32[]{:T(128)}, ...), branch_computations={%region_3.6_spmd, %region_7.7_spmd} | conditional | flops 137883904 | bytes 7108087 | solution.py:61
  82.7 26.0 %all-gather = f32[8,4,128]{2,1,0:T(4,128)S(1)} all-gather(f32[1,4,128]{2,1,0:T(4,128)S(1)} %convolution_bitcast_fusion.4), channel_id=1, replica_groups=mesh['seq'=8,'head'=4] {'seq'}, dimensions={0}, use_global_device_ids=true | all-gather | bytes 18432 | tf_op jit(solution)/shard_map/all_gather | solution.py:96
  110.2 8.3 %all-reduce = s32[32]{0:T(128)S(1)} all-reduce(s32[32]{0:T(128)S(1)} %dynamic-update-slice), channel_id=1, replica_groups=mesh['seq'=8,'head'=4] {'seq'}, use_global_device_ids=true, to_apply=%add | all-reduce | flops 32 | bytes 256
  121.0 36.3 %all-reduce.1 = f32[32,128]{1,0:T(8,128)S(1)} all-reduce(f32[32,128]{1,0:T(8,128)S(1)} %fusion.11), channel_id=2, replica_groups=mesh['seq'=8,'head'=4] {'seq'}, use_global_device_ids=true, to_apply=%region_27.28.clone | all-reduce | flops 4096 | bytes 32768
  160.5 36.9 %psum.21 = f32[]{:T(128)} all-reduce(f32[]{:T(128)S(6)} %div.35), channel_id=1, replica_groups=mesh['seq'=8,'head'=4] {'seq','head'}, use_global_device_ids=true, to_apply=%region_24.25 | all-reduce | flops 1 | bytes 8 | tf_op jit(solution)/shard_map/psum | solution.py:114
  197.4 30.8 %all-reduce.5.cloned.1.call-done = (f32[1,128,128]{2,1,0:T(8,128)}, f32[1,384,128]{2,1,0:T(8,128)}) async-done(((f32[1,128,128]{2,1,0:T(8,128)}, f32[1,384,128]{2,1,0:T(8,128)}), (f32[1,128,128]{2,1,0:T(8,128)}, f32[1,384,128]{2,1,0:T(8,128)})) %all-reduce.5.cloned.1.call-update) | async-done | bytes 262160 | tf_op jit(solution)/shard_map/psum | solution.py:113
  229.7 1.6 copy.71
  (190 shorter events, 55.2 us)
Async XLA Ops:
  7.2 75.4 %copy-start = (bf16[1,384,128]{2,1,0:T(8,128)(2,1)S(1)}, bf16[1,384,128]{2,1,0:T(8,128)(2,1)}, u32[]{:S(2)}) copy-start(bf16[1,384,128]{2,1,0:T(8,128)(2,1)} %param.15) | copy-start | bytes 294916
  7.2 4.7 %copy-start.4 = (s32[4]{0:T(128)S(1)}, s32[4]{0:T(128)}, u32[]{:S(2)}) copy-start(s32[4]{0:T(128)} %param.13) | copy-start | bytes 52
  7.2 221.0 %all-reduce.5.cloned.1.call-start = ((), (), s32[]{:S(2)}) async-start(), calls=%async_computation | async-start | bytes 524288 | tf_op jit(solution)/shard_map/psum | solution.py:113
  12.5 10.3 %collective-permute-start = (bf16[4,64,128]{2,1,0:T(8,128)(2,1)}, bf16[4,64,128]{2,1,0:T(8,128)(2,1)S(1)}, u32[]{:S(2)}, u32[]{:S(2)}) collective-permute-start(bf16[4,64,128]{2,1,0:T(8,128)(2,1)} %copy.52), channel_id=1, source_target_pairs={{28,0},{0,4},{4,8},{8,12},{12,16},{16,20},{20,24},{24,28},{29,1},{... | collective-permute-start | bytes 196616 | tf_op jit(solution)/shard_map/while/body/eval_jaxpr/ppermute | solution.py:17
  16.0 6.9 %collective-permute-start.1 = (s32[4]{0:T(128)}, s32[4]{0:T(128)S(1)}, u32[]{:S(2)}, u32[]{:S(2)}) collective-permute-start(s32[4]{0:T(128)} %copy.53), channel_id=1, source_target_pairs={{28,0},{0,4},{4,8},{8,12},{12,16},{16,20},{20,24},{24,28},{29,1},{... | collective-permute-start | bytes 56 | tf_op jit(solution)/shard_map/while/body/eval_jaxpr/ppermute | solution.py:17
  23.5 8.9 %collective-permute-start = (bf16[4,64,128]{2,1,0:T(8,128)(2,1)}, bf16[4,64,128]{2,1,0:T(8,128)(2,1)S(1)}, u32[]{:S(2)}, u32[]{:S(2)}) collective-permute-start(bf16[4,64,128]{2,1,0:T(8,128)(2,1)} %copy.52), channel_id=1, source_target_pairs={{28,0},{0,4},{4,8},{8,12},{12,16},{16,20},{20,24},{24,28},{29,1},{... | collective-permute-start | bytes 196616 | tf_op jit(solution)/shard_map/while/body/eval_jaxpr/ppermute | solution.py:17
  25.5 6.9 %collective-permute-start.1 = (s32[4]{0:T(128)}, s32[4]{0:T(128)S(1)}, u32[]{:S(2)}, u32[]{:S(2)}) collective-permute-start(s32[4]{0:T(128)} %copy.53), channel_id=1, source_target_pairs={{28,0},{0,4},{4,8},{8,12},{12,16},{16,20},{20,24},{24,28},{29,1},{... | collective-permute-start | bytes 56 | tf_op jit(solution)/shard_map/while/body/eval_jaxpr/ppermute | solution.py:17
  33.0 8.9 %collective-permute-start = (bf16[4,64,128]{2,1,0:T(8,128)(2,1)}, bf16[4,64,128]{2,1,0:T(8,128)(2,1)S(1)}, u32[]{:S(2)}, u32[]{:S(2)}) collective-permute-start(bf16[4,64,128]{2,1,0:T(8,128)(2,1)} %copy.52), channel_id=1, source_target_pairs={{28,0},{0,4},{4,8},{8,12},{12,16},{16,20},{20,24},{24,28},{29,1},{... | collective-permute-start | bytes 196616 | tf_op jit(solution)/shard_map/while/body/eval_jaxpr/ppermute | solution.py:17
  35.0 6.9 %collective-permute-start.1 = (s32[4]{0:T(128)}, s32[4]{0:T(128)S(1)}, u32[]{:S(2)}, u32[]{:S(2)}) collective-permute-start(s32[4]{0:T(128)} %copy.53), channel_id=1, source_target_pairs={{28,0},{0,4},{4,8},{8,12},{12,16},{16,20},{20,24},{24,28},{29,1},{... | collective-permute-start | bytes 56 | tf_op jit(solution)/shard_map/while/body/eval_jaxpr/ppermute | solution.py:17
  42.5 8.4 %collective-permute-start = (bf16[4,64,128]{2,1,0:T(8,128)(2,1)}, bf16[4,64,128]{2,1,0:T(8,128)(2,1)S(1)}, u32[]{:S(2)}, u32[]{:S(2)}) collective-permute-start(bf16[4,64,128]{2,1,0:T(8,128)(2,1)} %copy.52), channel_id=1, source_target_pairs={{28,0},{0,4},{4,8},{8,12},{12,16},{16,20},{20,24},{24,28},{29,1},{... | collective-permute-start | bytes 196616 | tf_op jit(solution)/shard_map/while/body/eval_jaxpr/ppermute | solution.py:17
  44.5 6.4 %collective-permute-start.1 = (s32[4]{0:T(128)}, s32[4]{0:T(128)S(1)}, u32[]{:S(2)}, u32[]{:S(2)}) collective-permute-start(s32[4]{0:T(128)} %copy.53), channel_id=1, source_target_pairs={{28,0},{0,4},{4,8},{8,12},{12,16},{16,20},{20,24},{24,28},{29,1},{... | collective-permute-start | bytes 56 | tf_op jit(solution)/shard_map/while/body/eval_jaxpr/ppermute | solution.py:17
  51.6 8.0 %collective-permute-start = (bf16[4,64,128]{2,1,0:T(8,128)(2,1)}, bf16[4,64,128]{2,1,0:T(8,128)(2,1)S(1)}, u32[]{:S(2)}, u32[]{:S(2)}) collective-permute-start(bf16[4,64,128]{2,1,0:T(8,128)(2,1)} %copy.52), channel_id=1, source_target_pairs={{28,0},{0,4},{4,8},{8,12},{12,16},{16,20},{20,24},{24,28},{29,1},{... | collective-permute-start | bytes 196616 | tf_op jit(solution)/shard_map/while/body/eval_jaxpr/ppermute | solution.py:17
  52.7 6.9 %collective-permute-start.1 = (s32[4]{0:T(128)}, s32[4]{0:T(128)S(1)}, u32[]{:S(2)}, u32[]{:S(2)}) collective-permute-start(s32[4]{0:T(128)} %copy.53), channel_id=1, source_target_pairs={{28,0},{0,4},{4,8},{8,12},{12,16},{16,20},{20,24},{24,28},{29,1},{... | collective-permute-start | bytes 56 | tf_op jit(solution)/shard_map/while/body/eval_jaxpr/ppermute | solution.py:17
  60.2 8.9 %collective-permute-start = (bf16[4,64,128]{2,1,0:T(8,128)(2,1)}, bf16[4,64,128]{2,1,0:T(8,128)(2,1)S(1)}, u32[]{:S(2)}, u32[]{:S(2)}) collective-permute-start(bf16[4,64,128]{2,1,0:T(8,128)(2,1)} %copy.52), channel_id=1, source_target_pairs={{28,0},{0,4},{4,8},{8,12},{12,16},{16,20},{20,24},{24,28},{29,1},{... | collective-permute-start | bytes 196616 | tf_op jit(solution)/shard_map/while/body/eval_jaxpr/ppermute | solution.py:17
  62.2 6.9 %collective-permute-start.1 = (s32[4]{0:T(128)}, s32[4]{0:T(128)S(1)}, u32[]{:S(2)}, u32[]{:S(2)}) collective-permute-start(s32[4]{0:T(128)} %copy.53), channel_id=1, source_target_pairs={{28,0},{0,4},{4,8},{8,12},{12,16},{16,20},{20,24},{24,28},{29,1},{... | collective-permute-start | bytes 56 | tf_op jit(solution)/shard_map/while/body/eval_jaxpr/ppermute | solution.py:17
  69.8 8.9 %collective-permute-start = (bf16[4,64,128]{2,1,0:T(8,128)(2,1)}, bf16[4,64,128]{2,1,0:T(8,128)(2,1)S(1)}, u32[]{:S(2)}, u32[]{:S(2)}) collective-permute-start(bf16[4,64,128]{2,1,0:T(8,128)(2,1)} %copy.52), channel_id=1, source_target_pairs={{28,0},{0,4},{4,8},{8,12},{12,16},{16,20},{20,24},{24,28},{29,1},{... | collective-permute-start | bytes 196616 | tf_op jit(solution)/shard_map/while/body/eval_jaxpr/ppermute | solution.py:17
  71.8 6.9 %collective-permute-start.1 = (s32[4]{0:T(128)}, s32[4]{0:T(128)S(1)}, u32[]{:S(2)}, u32[]{:S(2)}) collective-permute-start(s32[4]{0:T(128)} %copy.53), channel_id=1, source_target_pairs={{28,0},{0,4},{4,8},{8,12},{12,16},{16,20},{20,24},{24,28},{29,1},{... | collective-permute-start | bytes 56 | tf_op jit(solution)/shard_map/while/body/eval_jaxpr/ppermute | solution.py:17
  81.9 26.9 %copy-start.2 = (u32[32]{0:T(128)S(1)}, u32[32]{0:T(128)}, u32[]{:S(2)}) copy-start(u32[32]{0:T(128)} %constant.258) | copy-start | bytes 388
  81.9 28.1 %copy-start.3 = (s32[4]{0:T(128)S(1)}, s32[4]{0:T(128)}, u32[]{:S(2)}) copy-start(s32[4]{0:T(128)} %param.13) | copy-start | bytes 52
  81.9 36.7 %copy-start.1 = (bf16[1,128,128]{2,1,0:T(8,128)(2,1)S(1)}, bf16[1,128,128]{2,1,0:T(8,128)(2,1)}, u32[]{:S(2)}) copy-start(bf16[1,128,128]{2,1,0:T(8,128)(2,1)} %param.14) | copy-start | bytes 98308
Sparse Core Ops, SparseCore 0:
  160.0 68.1 all-reduce.4
where the time goes:
time: 239 us; the launch traced here: 238 us
  blocking collectives  108 us (45%)
  waiting for transfers between devices  32 us (13%)
  other arithmetic  22.7 us (9%)
  starting transfers between devices  20.3 us (8%)
  between operations  17.5 us (7%)
  local copies, waits for them, and re-layouts  15.3 us (6%)
  matrix products  12.7 us (5%)
  loops' own time  10.2 us (4%)
    unnamed x2, blocking collectives  44.6 us
    psum x1, blocking collectives, shards(): loss = lax.psum(loss_part, ('seq', 'head'))  36.9 us
    psum x1, waiting for transfers between devices, shards(): grad_q, grad_k = lax.psum((grad_q, grad_k), 'seq')  30.8 us
    all_gather x1, blocking collectives, shards(): lax.all_gather(kproj_own, 'seq', axis=0, tiled=True)  26 us
    ppermute x14, starting transfers between devices, passed_along(): return lax.ppermute(block, axis, route)  20.3 us
    reduce_min x8, other arithmetic, one(): jnp.min(posp) * BLOCK > qlast  9.94 us
    dot_general x8, matrix products, work(): lax.dot_general(qmat, kblk, (((1,), (1,)), ((), ())), preferred_element_t...  9.91 us
    another operation x1, loops' own time, shards(): lax.fori_loop(0, seq_count - 1, turn, (init, key_blocks, block_order))  9.38 us
  transfers between devices with their start and end apart: 15, of which 2 were waited for; matrix products, arithmetic and copies ran while one was open for 13% of the time, Pallas kernels for 0%

commit v1 on v0

v1 whole, which is shorter than its diff:
```python
import functools
import math

import jax
import jax.numpy as jnp
from jax import lax
from jax.experimental import pallas as pl
from jax.experimental.pallas import tpu as pltpu
from jax.sharding import PartitionSpec as P

BLOCK = 64
MESH = pl.DeviceIdType.MESH
HIGH = lax.Precision.HIGHEST
F32 = jnp.float32
BF16 = jnp.bfloat16
MASKED = -1e30
NT = (((1,), (1,)), ((), ()))
TN = (((0,), (0,)), ((), ()))
LANES = 128
STEP = 8


def kernel(
    n, heads, group, order_ref, q_ref, k_ref, gq_ref, gk_ref,
    loss_ref, dq_ref, dk_ref,
    kbuf, bmax, bsum, ords, kmax, kmin, ksum, qpool, top, mbuf, lbuf,
    ksend, krecv, fsend, msend, mrecv, lsend, lrecv,
):
    tok, width = k_ref.shape
    rows = q_ref.shape[0]
    local = tok // BLOCK
    blocks = n * local
    span = BLOCK * group
    pair = 2 if n % 2 == 0 else 1
    far = n // pair
    scale = width ** (-0.5)
    k2 = scale * math.log2(math.e)
    me = lax.axis_index("seq")
    head = lax.axis_index("head")
    a, r = me // pair, me % pair
    partner = a * pair + (r + 1) % pair

    barrier = pltpu.get_barrier_semaphore()
    for k in range(1, n):
        pl.semaphore_signal(barrier, inc=1, device_id={"seq": (me + k) % n}, device_id_type=MESH)
    for k in range(1, heads):
        pl.semaphore_signal(barrier, inc=1, device_id={"head": (head + k) % heads}, device_id_type=MESH)

    kbuf[me, pl.ds(0, tok), :] = k_ref[...]
    row = lax.broadcasted_iota(jnp.int32, (16, width), 0)
    tail = jnp.zeros((16, width), F32)
    for i in range(local):
        tail = jnp.where(row == i, order_ref[i].astype(F32), tail)
    kbuf[me, pl.ds(tok, 16), :] = tail.astype(BF16)
    pl.semaphore_wait(barrier, n - 1 + heads - 1)

    def key_copy(slot, send, to):
        return pltpu.make_async_remote_copy(
            src_ref=kbuf.at[slot], dst_ref=kbuf.at[slot], send_sem=send, recv_sem=krecv.at[slot],
            device_id={"seq": to}, device_id_type=MESH,
        )

    sends = []
    for k in range(1, far):
        to = (a + k) % far * pair + r
        sends.append(key_copy(me, ksend.at[k], to))
    if pair == 2:
        sends.insert(1, key_copy(me, ksend.at[0], partner))
    for copy in sends:
        copy.start()

    def process(slot, own):
        data = kbuf[slot, pl.ds(0, tok), :].astype(F32)
        tail = kbuf[slot, pl.ds(tok, 16), :].astype(F32)
        for i in range(local):
            part = data[i * BLOCK:(i + 1) * BLOCK].reshape(BLOCK // 8, 8, width)
            at = slot * local + i
            kmax[at] = jnp.max(part, axis=0)
            kmin[at] = jnp.min(part, axis=0)
            ksum[at] = jnp.sum(part, axis=0)
            ords[at] = jnp.broadcast_to(tail[i:i + 1], (8, width))
        half = span // 2
        if own:
            ahead = lax.broadcasted_iota(jnp.int32, (BLOCK, half), 0) - (
                lax.broadcasted_iota(jnp.int32, (BLOCK, half), 1) // group
            )

        def columns(b, _):
            for part in range(2):
                cols = pl.ds(pl.multiple_of(b * span + part * half, half), half)
                scores = lax.dot_general(
                    kbuf[slot, pl.ds(0, tok), :], q_ref[cols, :], NT, preferred_element_type=F32
                )
                for i in range(local):
                    s = scores[i * BLOCK:(i + 1) * BLOCK]
                    if own:
                        limit = jnp.where(b == i, part * (BLOCK // 2), 2 * BLOCK)
                        s = jnp.where(ahead > limit, MASKED / k2, s)
                    s = s.reshape(BLOCK // 8, 8, half)
                    high = jnp.max(s, axis=0)
                    at = slot * local + i
                    bmax[at, :, cols] = high * k2
                    bsum[at, :, cols] = jnp.sum(jnp.exp2((s - high) * k2), axis=0)
            return 0

        lax.fori_loop(0, local, columns, 0)

    def wait_keys(slot):
        key_copy(slot, ksend.at[0], partner).wait_recv()

    process(me, True)
    forwards = []
    near = [(a - k + far) % far * pair for k in range(far)]
    order = []
    for k in range(1, far):
        slot = near[k] + r
        wait_keys(slot)
        if pair == 2:
            copy = key_copy(slot, fsend.at[k], partner)
            copy.start()
            forwards.append(copy)
            beside = near[k - 1] + (r + 1) % pair
            wait_keys(beside)
            process(beside, False)
        process(slot, False)
    if pair == 2:
        beside = near[far - 1] + (r + 1) % pair
        wait_keys(beside)
        process(beside, False)

    lane = lax.broadcasted_iota(jnp.int32, (1, LANES), 1)
    tiles = span // LANES

    def pool(b, carry):
        pooled, mine = carry
        here = order_ref[b].astype(F32)
        start = b * span

        def scores_of(c, t):
            cols = pl.ds(pl.multiple_of(start + t * LANES, LANES), LANES)
            return jnp.where(ords[c] > here, MASKED, bmax[c, :, cols]), cols

        def highest(step, high):
            for j in range(STEP):
                high = tuple(
                    jnp.maximum(high[t], scores_of(step * STEP + j, t)[0]) for t in range(tiles)
                )
            return high

        high = lax.fori_loop(
            0, blocks // STEP, highest, (jnp.full((8, LANES), MASKED, F32),) * tiles
        )
        high = [jnp.max(x, axis=0, keepdims=True) for x in high]

        def add(step, total):
            for j in range(STEP):
                out = []
                for t in range(tiles):
                    s, cols = scores_of(step * STEP + j, t)
                    out.append(total[t] + jnp.exp2(s - high[t]) * bsum[step * STEP + j, :, cols])
                total = tuple(out)
            return total

        total = lax.fori_loop(0, blocks // STEP, add, (jnp.zeros((8, LANES), F32),) * tiles)
        lse = [
            high[t] + jnp.log2(jnp.sum(total[t], axis=0, keepdims=True)) for t in range(tiles)
        ]

        def tops(step, _):
            for j in range(STEP):
                c = step * STEP + j
                best = scores_of(c, 0)[0] - lse[0]
                for t in range(1, tiles):
                    best = jnp.maximum(best, scores_of(c, t)[0] - lse[t])
                top[c] = best
            return 0

        lax.fori_loop(0, blocks // STEP, tops, 0)
        best = jnp.max(top[...], axis=1)
        shift = group
        while shift < LANES:
            best = jnp.maximum(best, pltpu.roll(best, shift, 1))
            shift *= 2
        here_lanes = lane // group == b
        qsum = jnp.sum(
            q_ref[pl.ds(pl.multiple_of(start, span), span), :].astype(F32).reshape(BLOCK, group, width),
            axis=0,
        )
        qpool[pl.ds(pl.multiple_of(b * group, group), group), :] = qsum * (1.0 / BLOCK)
        return jnp.where(here_lanes, best, pooled), jnp.where(here_lanes, here, mine)

    qpool[...] = jnp.zeros_like(qpool)
    pooled, mine = lax.fori_loop(
        0, local, pool, (jnp.zeros((blocks, LANES), F32), jnp.zeros((1, LANES), F32))
    )
    valid = lane < local * group
    pooled = jnp.exp2(pooled)
    target = pooled / jnp.sum(pooled, axis=0, keepdims=True)

    kpool = jnp.concatenate(
        [
            jnp.max(kmax[...], axis=1),
            jnp.min(kmin[...], axis=1),
            jnp.sum(ksum[...], axis=1) * (1.0 / BLOCK),
        ],
        axis=1,
    ).astype(BF16)
    qp = qpool[...].astype(BF16)
    kproj = jnp.dot(kpool, gk_ref[...], preferred_element_type=F32)
    qproj = jnp.dot(qp, gq_ref[...], preferred_element_type=F32)
    gscale = gq_ref.shape[1] ** (-0.5)
    logits = lax.dot_general(kproj, qproj, NT, precision=HIGH, preferred_element_type=F32) * gscale
    logits = jnp.where(ords[:, 0, :] > mine, MASKED, logits)
    shifted = logits - jnp.max(logits, axis=0, keepdims=True)
    weight = jnp.exp(shifted)
    norm = jnp.sum(weight, axis=0, keepdims=True)
    logp = shifted - jnp.log(norm)
    count = group * heads * blocks
    safe = jnp.log(jnp.where(target > 0, target, 1.0))
    terms = jnp.where((target > 0) & valid, target * (safe - logp), 0.0) * (1.0 / count)
    rowtot = jnp.sum(target, axis=0, keepdims=True)
    dlogit = jnp.where(valid, (weight / norm * rowtot - target) * (gscale / count), 0.0)
    mbuf[me, pl.ds(0, blocks), :] = jnp.dot(
        dlogit, qp.astype(F32), precision=HIGH, preferred_element_type=F32
    )
    mbuf[me, pl.ds(blocks, 8), :] = jnp.sum(terms.reshape(blocks // 8, 8, LANES), axis=0)

    def sum_copy(slot, k, to):
        return pltpu.make_async_remote_copy(
            src_ref=mbuf.at[slot], dst_ref=mbuf.at[slot], send_sem=msend.at[k], recv_sem=mrecv.at[slot],
            device_id={"seq": to}, device_id_type=MESH,
        )

    shares = [sum_copy(me, k, (me + k) % n) for k in range(1, n)]
    for copy in shares:
        copy.start()
    for k in range(1, n):
        sum_copy((me + k) % n, k, me).wait_recv()
    total = mbuf[0]
    for slot in range(1, n):
        total = total + mbuf[slot]

    lbuf[head] = total[blocks:]

    def loss_copy(slot, k, to):
        return pltpu.make_async_remote_copy(
            src_ref=lbuf.at[slot], dst_ref=lbuf.at[slot], send_sem=lsend.at[k], recv_sem=lrecv.at[slot],
            device_id={"head": to}, device_id_type=MESH,
        )

    losses = [loss_copy(head, k, (head + k) % heads) for k in range(1, heads)]
    for copy in losses:
        copy.start()
    grad = total[:blocks]
    dq_ref[...] = lax.dot_general(grad, kproj, TN, precision=HIGH, preferred_element_type=F32)
    dkproj = jnp.dot(grad, gq_ref[...].astype(F32), precision=HIGH, preferred_element_type=F32)
    dk_ref[...] = lax.dot_general(
        kpool.astype(F32), dkproj, TN, precision=HIGH, preferred_element_type=F32
    )
    for k in range(1, heads):
        loss_copy((head + k) % heads, k, head).wait_recv()
    loss = lbuf[0]
    for slot in range(1, heads):
        loss = loss + lbuf[slot]
    loss_ref[0, 0] = jnp.sum(loss)
    for copy in sends + forwards + shares + losses:
        copy.wait_send()


def solution(mesh):
    n, heads = mesh.shape["seq"], mesh.shape["head"]

    def shards(queries, keys, block_order, gate_query, gate_key):
        tok, group, width = queries.shape
        local = tok // BLOCK
        blocks = local * n
        dim = gate_query.shape[2]
        pooled = gate_key.shape[1]
        vmem = pl.BlockSpec(memory_space=pltpu.VMEM)
        smem = pl.BlockSpec(memory_space=pltpu.SMEM)
        dma = pltpu.SemaphoreType.DMA
        block_rows = pltpu.VMEM((blocks, 8, width), F32)
        loss, grad_q, grad_k = pl.pallas_call(
            functools.partial(kernel, n, heads, group),
            out_shape=(
                jax.ShapeDtypeStruct((1, 1), F32),
                jax.ShapeDtypeStruct((width, dim), F32),
                jax.ShapeDtypeStruct((pooled, dim), F32),
            ),
            in_specs=[smem, vmem, vmem, vmem, vmem],
            out_specs=(smem, vmem, vmem),
            scratch_shapes=[
                pltpu.VMEM((n, tok + 16, width), BF16),
                pltpu.VMEM((blocks, 8, tok * group), F32),
                pltpu.VMEM((blocks, 8, tok * group), F32),
                block_rows,
                block_rows,
                block_rows,
                block_rows,
                pltpu.VMEM((LANES, width), F32),
                block_rows,
                pltpu.VMEM((n, blocks + 8, width), F32),
                pltpu.VMEM((heads, 8, width), F32),
                dma((n,)), dma((n,)), dma((n,)), dma((n,)), dma((n,)), dma((heads,)), dma((heads,)),
            ],
            compiler_params=pltpu.CompilerParams(
                collective_id=0, has_side_effects=True, vmem_limit_bytes=48 << 20
            ),
        )(
            block_order,
            queries.reshape(tok * group, width),
            keys.reshape(tok, width),
            gate_query[0],
            gate_key[0],
        )
        return loss[0, 0], grad_q[None], grad_k[None]

    return jax.shard_map(
        shards,
        mesh=mesh,
        in_specs=(
            P("seq", "head", None),
            P("seq", "head", None),
            P("seq"),
            P("head", None, None),
            P("head", None, None),
        ),
        out_specs=(P(), P("head", None, None), P("head", None, None)),
        check_vma=False,
    )
```

time: 239 us -> 40.6 us (0.17)
  blocking collectives: 108 us -> 0 us
  Pallas kernels: 0 us -> 32.5 us
  waiting for transfers between devices: 32 us -> 0 us
  other arithmetic: 22.7 us -> 0 us
  starting transfers between devices: 20.3 us -> 0 us
  between operations: 17.5 us -> 2.34 us
  matrix products: 12.7 us -> 0 us
  loops' own time: 10.2 us -> 0 us
  local copies, waits for them, and re-layouts: 15.3 us -> 5.49 us
    unnamed x2 -> x0, blocking collectives: 44.6 us -> none
    psum x1 -> x0, blocking collectives: 36.9 us -> none  [shards(): loss = lax.psum(loss_part, ('seq', 'head'))]
    pallas_call x0 -> x1, Pallas kernels: none -> 32.5 us  [shards(): pl.pallas_call(functools.partial(kernel, n, heads, group), out_shape=(jax...]
    psum x1 -> x0, waiting for transfers between devices: 30.8 us -> none  [shards(): grad_q, grad_k = lax.psum((grad_q, grad_k), 'seq')]
    all_gather x1 -> x0, blocking collectives: 26 us -> none  [shards(): lax.all_gather(kproj_own, 'seq', axis=0, tiled=True)]
    ppermute x14 -> x0, starting transfers between devices: 20.3 us -> none  [passed_along(): return lax.ppermute(block, axis, route)]
    dot_general x15 -> x0, matrix products: 12.7 us -> none  [the longest x8 9.91 us: work(): lax.dot_general(qmat, kblk, (((1,), (1,)), ((), ())), preferred_element_t...]
    another operation x9 -> x0, loops' own time: 10.2 us -> none  [the longest x1 9.38 us: shards(): lax.fori_loop(0, seq_count - 1, turn, (init, key_blocks, block_order))]
  transfers between devices with their start and end apart: 15 -> 0, of which waited for: 2 -> 0; matrix products, arithmetic and copies ran while one was open for 13% -> 0% of each run, Pallas kernels for 0% -> 0%
where the time goes in v1:
time: 40.6 us; the launch traced here: 40.3 us
  Pallas kernels  32.5 us (80%)
  local copies, waits for them, and re-layouts  5.49 us (14%)
  between operations  2.34 us (6%)
    pallas_call x1, Pallas kernels, shards(): pl.pallas_call(functools.partial(kernel, n, heads, group), out_shape=(jax...  32.5 us
    unnamed x12, local copies, waits for them, and re-layouts  5.49 us

profile of v1, /device:TPU:0, one launch (start us, length us, event | category | flops | bytes accessed | tf_op | source)
XLA Modules:
  0.0 40.3 jit_solution(16737990261688434107)
XLA Ops:
  0.6 0.0 copy-start.4
  0.6 0.6 %copy-done.4 = s32[4]{0:T(128)S(1)} copy-done((s32[4]{0:T(128)S(1)}, s32[4]{0:T(128)}, u32[]{:S(2)}) %copy-start.4) | copy-done | bytes 40
  1.3 0.0 copy-start
  1.3 1.0 %copy-done = bf16[256,8,128]{2,1,0:T(8,128)(2,1)S(1)} copy-done((bf16[256,8,128]{2,1,0:T(8,128)(2,1)S(1)}, bf16[256,8,128]{2,1,0:T(8,128)(2,1)}, u32[]{:S(2)}) %copy-start) | copy-done | bytes 524312
  2.3 0.0 copy-start.1
  2.3 0.9 %copy-done.1 = bf16[1,384,128]{2,1,0:T(8,128)(2,1)S(1)} copy-done((bf16[1,384,128]{2,1,0:T(8,128)(2,1)S(1)}, bf16[1,384,128]{2,1,0:T(8,128)(2,1)}, u32[]{:S(2)}) %copy-start.1) | copy-done | bytes 98328
  3.2 0.0 copy-start.2
  3.2 0.8 %copy-done.2 = bf16[256,1,128]{2,0,1:T(8,128)(2,1)S(1)} copy-done((bf16[256,1,128]{2,0,1:T(8,128)(2,1)S(1)}, bf16[256,1,128]{2,0,1:T(8,128)(2,1)}, u32[]{:S(2)}) %copy-start.2) | copy-done | bytes 65560
  4.1 0.0 copy-start.3
  4.1 0.8 %copy-done.3 = bf16[1,128,128]{2,1,0:T(8,128)(2,1)S(1)} copy-done((bf16[1,128,128]{2,1,0:T(8,128)(2,1)S(1)}, bf16[1,128,128]{2,1,0:T(8,128)(2,1)}, u32[]{:S(2)}) %copy-start.3) | copy-done | bytes 32792
  4.8 32.5 %shard_map.76 = (f32[1,1]{1,0:T(1,128)}, f32[128,128]{1,0:T(8,128)S(1)}, f32[384,128]{1,0:T(8,128)S(1)}) custom-call(s32[4]{0:T(128)S(1)} %copy-done.4, bf16[2048,128]{1,0:T(8,128)(2,1)S(1)} %bitcast.7, bf16[256,128]{1,0:T(8,128)(2,1)S(1)} %bitcast.10, bf16[128,128]{1,0:T(8,128)(2,1)S(1)} %bitcast.12, bf16[384,128]{1,0:T(8,128)(2,1)S(1)} %bitcast.9), custom_call_target="tpu_custom_call" | custom-call | tf_op jit(solution)/shard_map/pallas_call | solution.py:283
  37.9 0.6 %copy.12 = f32[1,128,128]{2,1,0:T(8,128)} copy(f32[1,128,128]{2,1,0:T(8,128)S(1)} %bitcast.11) | data formatting | bytes 131072
  38.5 0.7 %copy.13 = f32[1,384,128]{2,1,0:T(8,128)} copy(f32[1,384,128]{2,1,0:T(8,128)S(1)} %bitcast.8) | data formatting | bytes 393216
Async XLA Ops:
  0.6 0.7 %copy-start.4 = (s32[4]{0:T(128)S(1)}, s32[4]{0:T(128)}, u32[]{:S(2)}) copy-start(s32[4]{0:T(128)} %order_ref.1) | copy-start | bytes 52
  1.3 1.0 %copy-start = (bf16[256,8,128]{2,1,0:T(8,128)(2,1)S(1)}, bf16[256,8,128]{2,1,0:T(8,128)(2,1)}, u32[]{:S(2)}) copy-start(bf16[256,8,128]{2,1,0:T(8,128)(2,1)} %param.5) | copy-start | bytes 1572868
  2.3 0.9 %copy-start.1 = (bf16[1,384,128]{2,1,0:T(8,128)(2,1)S(1)}, bf16[1,384,128]{2,1,0:T(8,128)(2,1)}, u32[]{:S(2)}) copy-start(bf16[1,384,128]{2,1,0:T(8,128)(2,1)} %param.9) | copy-start | bytes 294916
  3.2 0.8 %copy-start.2 = (bf16[256,1,128]{2,0,1:T(8,128)(2,1)S(1)}, bf16[256,1,128]{2,0,1:T(8,128)(2,1)}, u32[]{:S(2)}) copy-start(bf16[256,1,128]{2,0,1:T(8,128)(2,1)} %param.6) | copy-start | bytes 196612
  4.1 0.8 %copy-start.3 = (bf16[1,128,128]{2,1,0:T(8,128)(2,1)S(1)}, bf16[1,128,128]{2,1,0:T(8,128)(2,1)}, u32[]{:S(2)}) copy-start(bf16[1,128,128]{2,1,0:T(8,128)(2,1)} %param.8) | copy-start | bytes 98308

commit v2 on v1

--- a/solution.py
+++ b/solution.py
@@ -17,17 +17,17 @@
 NT = (((1,), (1,)), ((), ()))
 TN = (((0,), (0,)), ((), ()))
 LANES = 128
-STEP = 8
+STEP = 32
 
 
 def kernel(
-    n, heads, group, order_ref, q_ref, k_ref, gq_ref, gk_ref,
+    n, heads, group, order_hbm, q_hbm, k_hbm, gq_hbm, gk_hbm,
     loss_ref, dq_ref, dk_ref,
-    kbuf, bmax, bsum, ords, kmax, kmin, ksum, qpool, top, mbuf, lbuf,
-    ksend, krecv, fsend, msend, mrecv, lsend, lrecv,
+    kbuf, bmax, rmax, rsum, ords, kmax, kmin, ksum, top, mbuf, lbuf,
+    order_ref, q_ref, qt, gq_ref, gk_ref,
+    ksend, krecv, fsend, msend, mrecv, lsend, lrecv, held,
 ):
-    tok, width = k_ref.shape
-    rows = q_ref.shape[0]
+    tok, width = k_hbm.shape
     local = tok // BLOCK
     blocks = n * local
     span = BLOCK * group
@@ -46,12 +46,23 @@
     for k in range(1, heads):
         pl.semaphore_signal(barrier, inc=1, device_id={"head": (head + k) % heads}, device_id_type=MESH)
 
-    kbuf[me, pl.ds(0, tok), :] = k_ref[...]
+    fetch = [
+        pltpu.make_async_copy(k_hbm, kbuf.at[me, pl.ds(0, tok), :], held.at[0]),
+        pltpu.make_async_copy(order_hbm, order_ref, held.at[1]),
+        pltpu.make_async_copy(q_hbm, q_ref, held.at[2]),
+        pltpu.make_async_copy(gq_hbm, gq_ref, held.at[3]),
+        pltpu.make_async_copy(gk_hbm, gk_ref, held.at[4]),
+    ]
+    for copy in fetch:
+        copy.start()
+
+    fetch[1].wait()
     row = lax.broadcasted_iota(jnp.int32, (16, width), 0)
     tail = jnp.zeros((16, width), F32)
     for i in range(local):
         tail = jnp.where(row == i, order_ref[i].astype(F32), tail)
     kbuf[me, pl.ds(tok, 16), :] = tail.astype(BF16)
+    fetch[0].wait()
     pl.semaphore_wait(barrier, n - 1 + heads - 1)
 
     def key_copy(slot, send, to):
@@ -68,6 +79,22 @@
         sends.insert(1, key_copy(me, ksend.at[0], partner))
     for copy in sends:
         copy.start()
+
+    fetch[2].wait()
+    qpool = []
+    for b in range(local):
+        data = q_ref[pl.ds(b * span, span), :]
+        qt[:, pl.ds(b * span, span)] = data.T
+        qpool.append(jnp.sum(data.astype(F32).reshape(BLOCK, group, width), axis=0))
+    qpool.append(jnp.zeros((LANES - local * group, width), F32))
+    qp = (jnp.concatenate(qpool, axis=0) * (1.0 / BLOCK)).astype(BF16)
+    fetch[3].wait()
+    fetch[4].wait()
+    qproj = jnp.dot(qp, gq_ref[...], preferred_element_type=F32)
+    rmax[...] = jnp.full_like(rmax, MASKED)
+    rsum[...] = jnp.zeros_like(rsum)
+
+    half = span // 2
 
     def process(slot, own):
         data = kbuf[slot, pl.ds(0, tok), :].astype(F32)
@@ -79,31 +106,45 @@
             kmin[at] = jnp.min(part, axis=0)
             ksum[at] = jnp.sum(part, axis=0)
             ords[at] = jnp.broadcast_to(tail[i:i + 1], (8, width))
-        half = span // 2
         if own:
             ahead = lax.broadcasted_iota(jnp.int32, (BLOCK, half), 0) - (
                 lax.broadcasted_iota(jnp.int32, (BLOCK, half), 1) // group
             )
 
-        def columns(b, _):
-            for part in range(2):
-                cols = pl.ds(pl.multiple_of(b * span + part * half, half), half)
-                scores = lax.dot_general(
-                    kbuf[slot, pl.ds(0, tok), :], q_ref[cols, :], NT, preferred_element_type=F32
-                )
-                for i in range(local):
-                    s = scores[i * BLOCK:(i + 1) * BLOCK]
-                    if own:
-                        limit = jnp.where(b == i, part * (BLOCK // 2), 2 * BLOCK)
-                        s = jnp.where(ahead > limit, MASKED / k2, s)
-                    s = s.reshape(BLOCK // 8, 8, half)
-                    high = jnp.max(s, axis=0)
-                    at = slot * local + i
-                    bmax[at, :, cols] = high * k2
-                    bsum[at, :, cols] = jnp.sum(jnp.exp2((s - high) * k2), axis=0)
+        def tile(b, part):
+            cols = pl.ds(pl.multiple_of(b * span + part * half, half), half)
+            here = order_ref[b].astype(F32)
+            scores = jnp.dot(
+                kbuf[slot, pl.ds(0, tok), :], qt[:, cols], preferred_element_type=F32
+            )
+            highs, sums = [], []
+            for i in range(local):
+                s = scores[i * BLOCK:(i + 1) * BLOCK]
+                if own:
+                    limit = jnp.where(b == i, part * (BLOCK // 2), 2 * BLOCK)
+                    s = jnp.where(ahead > limit, MASKED / k2, s)
+                s = s.reshape(BLOCK // 8, 8, half)
+                high = jnp.max(s, axis=0)
+                sums.append(jnp.sum(jnp.exp2((s - high) * k2), axis=0))
+                later = jnp.broadcast_to(tail[i:i + 1, :1], (8, half)) > here
+                high = jnp.where(later, MASKED, high * k2)
+                bmax[slot * local + i, :, cols] = high
+                highs.append(high)
+            old = rmax[:, cols]
+            new = functools.reduce(jnp.maximum, highs, old)
+            total = rsum[:, cols] * jnp.exp2(old - new)
+            for high, amount in zip(highs, sums):
+                total = total + amount * jnp.exp2(high - new)
+            rmax[:, cols] = new
+            rsum[:, cols] = total
+
+        def columns(step, _):
+            for b in range(2):
+                for part in range(2):
+                    tile(step * 2 + b, part)
             return 0
 
-        lax.fori_loop(0, local, columns, 0)
+        lax.fori_loop(0, local // 2, columns, 0)
 
     def wait_keys(slot):
         key_copy(slot, ksend.at[0], partner).wait_recv()
@@ -111,7 +152,6 @@
     process(me, True)
     forwards = []
     near = [(a - k + far) % far * pair for k in range(far)]
-    order = []
     for k in range(1, far):
         slot = near[k] + r
         wait_keys(slot)
@@ -128,75 +168,6 @@
         wait_keys(beside)
         process(beside, False)
 
-    lane = lax.broadcasted_iota(jnp.int32, (1, LANES), 1)
-    tiles = span // LANES
-
-    def pool(b, carry):
-        pooled, mine = carry
-        here = order_ref[b].astype(F32)
-        start = b * span
-
-        def scores_of(c, t):
-            cols = pl.ds(pl.multiple_of(start + t * LANES, LANES), LANES)
-            return jnp.where(ords[c] > here, MASKED, bmax[c, :, cols]), cols
-
-        def highest(step, high):
-            for j in range(STEP):
-                high = tuple(
-                    jnp.maximum(high[t], scores_of(step * STEP + j, t)[0]) for t in range(tiles)
-                )
-            return high
-
-        high = lax.fori_loop(
-            0, blocks // STEP, highest, (jnp.full((8, LANES), MASKED, F32),) * tiles
-        )
-        high = [jnp.max(x, axis=0, keepdims=True) for x in high]
-
-        def add(step, total):
-            for j in range(STEP):
-                out = []
-                for t in range(tiles):
-                    s, cols = scores_of(step * STEP + j, t)
-                    out.append(total[t] + jnp.exp2(s - high[t]) * bsum[step * STEP + j, :, cols])
-                total = tuple(out)
-            return total
-
-        total = lax.fori_loop(0, blocks // STEP, add, (jnp.zeros((8, LANES), F32),) * tiles)
-        lse = [
-            high[t] + jnp.log2(jnp.sum(total[t], axis=0, keepdims=True)) for t in range(tiles)
-        ]
-
-        def tops(step, _):
-            for j in range(STEP):
-                c = step * STEP + j
-                best = scores_of(c, 0)[0] - lse[0]
-                for t in range(1, tiles):
-                    best = jnp.maximum(best, scores_of(c, t)[0] - lse[t])
-                top[c] = best
-            return 0
-
-        lax.fori_loop(0, blocks // STEP, tops, 0)
-        best = jnp.max(top[...], axis=1)
-        shift = group
-        while shift < LANES:
-            best = jnp.maximum(best, pltpu.roll(best, shift, 1))
-            shift *= 2
-        here_lanes = lane // group == b
-        qsum = jnp.sum(
-            q_ref[pl.ds(pl.multiple_of(start, span), span), :].astype(F32).reshape(BLOCK, group, width),
-            axis=0,
-        )
-        qpool[pl.ds(pl.multiple_of(b * group, group), group), :] = qsum * (1.0 / BLOCK)
-        return jnp.where(here_lanes, best, pooled), jnp.where(here_lanes, here, mine)
-
-    qpool[...] = jnp.zeros_like(qpool)
-    pooled, mine = lax.fori_loop(
-        0, local, pool, (jnp.zeros((blocks, LANES), F32), jnp.zeros((1, LANES), F32))
-    )
-    valid = lane < local * group
-    pooled = jnp.exp2(pooled)
-    target = pooled / jnp.sum(pooled, axis=0, keepdims=True)
-
     kpool = jnp.concatenate(
         [
             jnp.max(kmax[...], axis=1),
@@ -205,9 +176,43 @@
         ],
         axis=1,
     ).astype(BF16)
-    qp = qpool[...].astype(BF16)
     kproj = jnp.dot(kpool, gk_ref[...], preferred_element_type=F32)
-    qproj = jnp.dot(qp, gq_ref[...], preferred_element_type=F32)
+
+    lane = lax.broadcasted_iota(jnp.int32, (1, LANES), 1)
+    tiles = span // LANES
+    pooled = jnp.zeros((blocks, LANES), F32)
+    mine = jnp.zeros((1, LANES), F32)
+    for b in range(local):
+        lse = []
+        for t in range(tiles):
+            cols = pl.ds(b * span + t * LANES, LANES)
+            part = rmax[:, cols]
+            high = jnp.max(part, axis=0, keepdims=True)
+            total = jnp.sum(rsum[:, cols] * jnp.exp2(part - high), axis=0, keepdims=True)
+            lse.append(high + jnp.log2(total))
+
+        def tops(step, _):
+            for j in range(STEP):
+                c = step * STEP + j
+                best = [
+                    bmax[c, :, pl.ds(b * span + t * LANES, LANES)] - lse[t] for t in range(tiles)
+                ]
+                top[b, c] = functools.reduce(jnp.maximum, best)
+            return 0
+
+        lax.fori_loop(0, blocks // STEP, tops, 0)
+        best = jnp.max(top[b], axis=1)
+        shift = group
+        while shift < LANES:
+            best = jnp.maximum(best, pltpu.roll(best, shift, 1))
+            shift *= 2
+        here_lanes = lane // group == b
+        pooled = jnp.where(here_lanes, best, pooled)
+        mine = jnp.where(here_lanes, order_ref[b].astype(F32), mine)
+    valid = lane < local * group
+    pooled = jnp.exp2(pooled)
+    target = pooled / jnp.sum(pooled, axis=0, keepdims=True)
+
     gscale = gq_ref.shape[1] ** (-0.5)
     logits = lax.dot_general(kproj, qproj, NT, precision=HIGH, preferred_element_type=F32) * gscale
     logits = jnp.where(ords[:, 0, :] > mine, MASKED, logits)
@@ -277,6 +282,7 @@
         dim = gate_query.shape[2]
         pooled = gate_key.shape[1]
         vmem = pl.BlockSpec(memory_space=pltpu.VMEM)
+        hbm = pl.BlockSpec(memory_space=pltpu.HBM)
         smem = pl.BlockSpec(memory_space=pltpu.SMEM)
         dma = pltpu.SemaphoreType.DMA
         block_rows = pltpu.VMEM((blocks, 8, width), F32)
@@ -287,24 +293,29 @@
                 jax.ShapeDtypeStruct((width, dim), F32),
                 jax.ShapeDtypeStruct((pooled, dim), F32),
             ),
-            in_specs=[smem, vmem, vmem, vmem, vmem],
+            in_specs=[hbm] * 5,
             out_specs=(smem, vmem, vmem),
             scratch_shapes=[
                 pltpu.VMEM((n, tok + 16, width), BF16),
                 pltpu.VMEM((blocks, 8, tok * group), F32),
-                pltpu.VMEM((blocks, 8, tok * group), F32),
+                pltpu.VMEM((8, tok * group), F32),
+                pltpu.VMEM((8, tok * group), F32),
                 block_rows,
                 block_rows,
                 block_rows,
                 block_rows,
-                pltpu.VMEM((LANES, width), F32),
-                block_rows,
+                pltpu.VMEM((local, blocks, 8, width), F32),
                 pltpu.VMEM((n, blocks + 8, width), F32),
                 pltpu.VMEM((heads, 8, width), F32),
-                dma((n,)), dma((n,)), dma((n,)), dma((n,)), dma((n,)), dma((heads,)), dma((heads,)),
+                pltpu.SMEM((local,), jnp.int32),
+                pltpu.VMEM((tok * group, width), BF16),
+                pltpu.VMEM((width, tok * group), BF16),
+                pltpu.VMEM((width, dim), BF16),
+                pltpu.VMEM((pooled, dim), BF16),
+                dma((n,)), dma((n,)), dma((n,)), dma((n,)), dma((n,)), dma((heads,)), dma((heads,)), dma((5,)),
             ],
             compiler_params=pltpu.CompilerParams(
-                collective_id=0, has_side_effects=True, vmem_limit_bytes=48 << 20
+                collective_id=0, has_side_effects=True, vmem_limit_bytes=64 << 20
             ),
         )(
             block_order,

time: 40.6 us -> 34.5 us (0.85)
  Pallas kernels: 32.5 us -> 28.8 us
  local copies, waits for them, and re-layouts: 5.49 us -> 3.09 us
    pallas_call x1, Pallas kernels: 32.5 us -> 28.8 us  [shards(): pl.pallas_call(functools.partial(kernel, n, heads, group), out_shape=(jax...]
    unnamed x12 -> x2, local copies, waits for them, and re-layouts: 5.49 us -> 3.09 us
where the time goes in v2:
time: 34.5 us; the launch traced here: 34.3 us
  Pallas kernels  28.8 us (83%)
  local copies, waits for them, and re-layouts  3.09 us (9%)
  between operations  2.4 us (7%)
    pallas_call x1, Pallas kernels, shards(): pl.pallas_call(functools.partial(kernel, n, heads, group), out_shape=(jax...  28.8 us
    unnamed x2, local copies, waits for them, and re-layouts  3.09 us

profile of v2, /device:TPU:0, one launch (start us, length us, event | category | flops | bytes accessed | tf_op | source)
XLA Modules:
  0.0 34.3 jit_solution(913596269418797141)
XLA Ops:
  0.6 28.8 %shard_map.76 = (f32[1,1]{1,0:T(1,128)}, f32[128,128]{1,0:T(8,128)}, f32[384,128]{1,0:T(8,128)}) custom-call(s32[4]{0:T(128)} %order_hbm.1, bf16[2048,128]{1,0:T(8,128)(2,1)} %bitcast.7, bf16[256,128]{1,0:T(8,128)(2,1)} %bitcast.10, bf16[128,128]{1,0:T(8,128)(2,1)} %bitcast.12, bf16[384,128]{1,0:T(8,128)(2,1)} %bitcast.9), custom_call_target="tpu_custom_call" | custom-call | tf_op jit(solution)/shard_map/pallas_call | solution.py:289
  30.0 1.5 %copy.12 = f32[1,128,128]{2,1,0:T(8,128)} copy(f32[1,128,128]{2,1,0:T(8,128)} %bitcast.11) | data formatting | bytes 131072
  31.5 1.6 %copy.13 = f32[1,384,128]{2,1,0:T(8,128)} copy(f32[1,384,128]{2,1,0:T(8,128)} %bitcast.8) | data formatting | bytes 393216

commit v3 on v2

--- a/solution.py
+++ b/solution.py
@@ -23,22 +23,22 @@
 def kernel(
     n, heads, group, order_hbm, q_hbm, k_hbm, gq_hbm, gk_hbm,
     loss_ref, dq_ref, dk_ref,
-    kbuf, bmax, rmax, rsum, ords, kmax, kmin, ksum, top, mbuf, lbuf,
+    kbuf, bmax, rmax, rsum, ords, kmax, kmin, kmean, top, mbuf, lbuf,
     order_ref, q_ref, qt, gq_ref, gk_ref,
     ksend, krecv, fsend, msend, mrecv, lsend, lrecv, held,
 ):
     tok, width = k_hbm.shape
     local = tok // BLOCK
+    extra = kbuf.shape[1] - tok
     blocks = n * local
     span = BLOCK * group
-    pair = 2 if n % 2 == 0 else 1
-    far = n // pair
+    far = n // 2
     scale = width ** (-0.5)
     k2 = scale * math.log2(math.e)
     me = lax.axis_index("seq")
     head = lax.axis_index("head")
-    a, r = me // pair, me % pair
-    partner = a * pair + (r + 1) % pair
+    a, r = me // 2, me % 2
+    partner = a * 2 + (r + 1) % 2
 
     barrier = pltpu.get_barrier_semaphore()
     for k in range(1, n):
@@ -57,12 +57,20 @@
         copy.start()
 
     fetch[1].wait()
-    row = lax.broadcasted_iota(jnp.int32, (16, width), 0)
-    tail = jnp.zeros((16, width), F32)
+    fetch[0].wait()
+    row = lax.broadcasted_iota(jnp.int32, (extra, width), 0)
+    tail = jnp.zeros((extra, width), F32)
     for i in range(local):
-        tail = jnp.where(row == i, order_ref[i].astype(F32), tail)
-    kbuf[me, pl.ds(tok, 16), :] = tail.astype(BF16)
-    fetch[0].wait()
+        part = kbuf[me, pl.ds(i * BLOCK, BLOCK), :].astype(F32).reshape(BLOCK // 8, 8, width)
+        pieces = (
+            order_ref[i].astype(F32),
+            jnp.max(jnp.max(part, axis=0), axis=0, keepdims=True),
+            jnp.min(jnp.min(part, axis=0), axis=0, keepdims=True),
+            jnp.sum(jnp.sum(part, axis=0), axis=0, keepdims=True) * (1.0 / BLOCK),
+        )
+        for m, piece in enumerate(pieces):
+            tail = jnp.where(row == 4 * i + m, piece, tail)
+    kbuf[me, pl.ds(tok, extra), :] = tail.astype(BF16)
     pl.semaphore_wait(barrier, n - 1 + heads - 1)
 
     def key_copy(slot, send, to):
@@ -73,10 +81,9 @@
 
     sends = []
     for k in range(1, far):
-        to = (a + k) % far * pair + r
+        to = (a + k) % far * 2 + r
         sends.append(key_copy(me, ksend.at[k], to))
-    if pair == 2:
-        sends.insert(1, key_copy(me, ksend.at[0], partner))
+    sends.insert(1, key_copy(me, ksend.at[0], partner))
     for copy in sends:
         copy.start()
 
@@ -96,86 +103,68 @@
 
     half = span // 2
 
-    def process(slot, own):
-        data = kbuf[slot, pl.ds(0, tok), :].astype(F32)
-        tail = kbuf[slot, pl.ds(tok, 16), :].astype(F32)
-        for i in range(local):
-            part = data[i * BLOCK:(i + 1) * BLOCK].reshape(BLOCK // 8, 8, width)
-            at = slot * local + i
-            kmax[at] = jnp.max(part, axis=0)
-            kmin[at] = jnp.min(part, axis=0)
-            ksum[at] = jnp.sum(part, axis=0)
-            ords[at] = jnp.broadcast_to(tail[i:i + 1], (8, width))
-        if own:
-            ahead = lax.broadcasted_iota(jnp.int32, (BLOCK, half), 0) - (
-                lax.broadcasted_iota(jnp.int32, (BLOCK, half), 1) // group
-            )
-
-        def tile(b, part):
-            cols = pl.ds(pl.multiple_of(b * span + part * half, half), half)
-            here = order_ref[b].astype(F32)
-            scores = jnp.dot(
-                kbuf[slot, pl.ds(0, tok), :], qt[:, cols], preferred_element_type=F32
-            )
-            highs, sums = [], []
-            for i in range(local):
-                s = scores[i * BLOCK:(i + 1) * BLOCK]
-                if own:
-                    limit = jnp.where(b == i, part * (BLOCK // 2), 2 * BLOCK)
-                    s = jnp.where(ahead > limit, MASKED / k2, s)
-                s = s.reshape(BLOCK // 8, 8, half)
-                high = jnp.max(s, axis=0)
-                sums.append(jnp.sum(jnp.exp2((s - high) * k2), axis=0))
-                later = jnp.broadcast_to(tail[i:i + 1, :1], (8, half)) > here
-                high = jnp.where(later, MASKED, high * k2)
-                bmax[slot * local + i, :, cols] = high
-                highs.append(high)
-            old = rmax[:, cols]
-            new = functools.reduce(jnp.maximum, highs, old)
-            total = rsum[:, cols] * jnp.exp2(old - new)
-            for high, amount in zip(highs, sums):
-                total = total + amount * jnp.exp2(high - new)
-            rmax[:, cols] = new
-            rsum[:, cols] = total
-
-        def columns(step, _):
-            for b in range(2):
-                for part in range(2):
-                    tile(step * 2 + b, part)
-            return 0
-
-        lax.fori_loop(0, local // 2, columns, 0)
+    ahead = lax.broadcasted_iota(jnp.int32, (BLOCK, half), 0) - (
+        lax.broadcasted_iota(jnp.int32, (BLOCK, half), 1) // group
+    )
 
     def wait_keys(slot):
         key_copy(slot, ksend.at[0], partner).wait_recv()
 
-    process(me, True)
-    forwards = []
-    near = [(a - k + far) % far * pair for k in range(far)]
-    for k in range(1, far):
-        slot = near[k] + r
-        wait_keys(slot)
-        if pair == 2:
-            copy = key_copy(slot, fsend.at[k], partner)
-            copy.start()
-            forwards.append(copy)
-            beside = near[k - 1] + (r + 1) % pair
-            wait_keys(beside)
-            process(beside, False)
-        process(slot, False)
-    if pair == 2:
-        beside = near[far - 1] + (r + 1) % pair
-        wait_keys(beside)
-        process(beside, False)
-
-    kpool = jnp.concatenate(
-        [
-            jnp.max(kmax[...], axis=1),
-            jnp.min(kmin[...], axis=1),
-            jnp.sum(ksum[...], axis=1) * (1.0 / BLOCK),
-        ],
-        axis=1,
-    ).astype(BF16)
+    def shard(j, _):
+        back = j // 2
+        slot = (a - back + far) % far * 2 + (r + j) % 2
+
+        @pl.when((j % 2 == 1) & (back + 1 < far))
+        def _():
+            direct = (a - back - 1 + far) % far * 2 + r
+            wait_keys(direct)
+            key_copy(direct, fsend.at[back + 1], partner).start()
+
+        @pl.when(j % 2 == 1)
+        def _():
+            wait_keys(slot)
+
+        tail = kbuf[slot, pl.ds(tok, extra), :].astype(F32)
+        for i in range(local):
+            at = slot * local + i
+            for m, ref in enumerate((ords, kmax, kmin, kmean)):
+                ref[at] = jnp.broadcast_to(tail[4 * i + m:4 * i + m + 1], (8, width))
+        unmasked = jnp.where(j == 0, 0, 2 * BLOCK)
+
+        for b in range(local):
+            here = order_ref[b].astype(F32)
+            for part in range(2):
+                cols = pl.ds(b * span + part * half, half)
+                scores = jnp.dot(
+                    kbuf[slot, pl.ds(0, tok), :], qt[:, cols], preferred_element_type=F32
+                )
+                highs, sums = [], []
+                for i in range(local):
+                    s = scores[i * BLOCK:(i + 1) * BLOCK]
+                    if b == i:
+                        s = jnp.where(ahead > unmasked + part * (BLOCK // 2), MASKED / k2, s)
+                    s = s.reshape(BLOCK // 8, 8, half)
+                    high = jnp.max(s, axis=0)
+                    sums.append(jnp.sum(jnp.exp2((s - high) * k2), axis=0))
+                    later = jnp.broadcast_to(tail[4 * i:4 * i + 1, :1], (8, half)) > here
+                    high = jnp.where(later, MASKED, high * k2)
+                    bmax[slot * local + i, :, cols] = high
+                    highs.append(high)
+                old = rmax[:, cols]
+                new = functools.reduce(jnp.maximum, highs, old)
+                total = rsum[:, cols] * jnp.exp2(old - new)
+                for high, amount in zip(highs, sums):
+                    total = total + amount * jnp.exp2(high - new)
+                rmax[:, cols] = new
+                rsum[:, cols] = total
+        return 0
+
+    lax.fori_loop(0, n, shard, 0)
+    forwards = [
+        key_copy((a - k + far) % far * 2 + r, fsend.at[k], partner) for k in range(1, far)
+    ]
+
+    kpool = jnp.concatenate([ref[:, 0, :] for ref in (kmax, kmin, kmean)], axis=1).astype(BF16)
     kproj = jnp.dot(kpool, gk_ref[...], preferred_element_type=F32)
 
     lane = lax.broadcasted_iota(jnp.int32, (1, LANES), 1)
@@ -279,6 +268,7 @@
         tok, group, width = queries.shape
         local = tok // BLOCK
         blocks = local * n
+        extra = -(-4 * local // 16) * 16
         dim = gate_query.shape[2]
         pooled = gate_key.shape[1]
         vmem = pl.BlockSpec(memory_space=pltpu.VMEM)
@@ -290,13 +280,13 @@
             functools.partial(kernel, n, heads, group),
             out_shape=(
                 jax.ShapeDtypeStruct((1, 1), F32),
-                jax.ShapeDtypeStruct((width, dim), F32),
-                jax.ShapeDtypeStruct((pooled, dim), F32),
+                pltpu.VMEM((width, dim), F32),
+                pltpu.VMEM((pooled, dim), F32),
             ),
             in_specs=[hbm] * 5,
             out_specs=(smem, vmem, vmem),
             scratch_shapes=[
-                pltpu.VMEM((n, tok + 16, width), BF16),
+                pltpu.VMEM((n, tok + extra, width), BF16),
                 pltpu.VMEM((blocks, 8, tok * group), F32),
                 pltpu.VMEM((8, tok * group), F32),
                 pltpu.VMEM((8, tok * group), F32),
@@ -315,14 +305,19 @@
                 dma((n,)), dma((n,)), dma((n,)), dma((n,)), dma((n,)), dma((heads,)), dma((heads,)), dma((5,)),
             ],
             compiler_params=pltpu.CompilerParams(
-                collective_id=0, has_side_effects=True, vmem_limit_bytes=64 << 20
+                collective_id=0, has_side_effects=True, vmem_limit_bytes=48 << 20
             ),
         )(
-            block_order,
-            queries.reshape(tok * group, width),
-            keys.reshape(tok, width),
-            gate_query[0],
-            gate_key[0],
+            *(
+                pltpu.with_memory_space_constraint(x, pltpu.HBM)
+                for x in (
+                    block_order,
+                    queries.reshape(tok * group, width),
+                    keys.reshape(tok, width),
+                    gate_query[0],
+                    gate_key[0],
+                )
+            )
         )
         return loss[0, 0], grad_q[None], grad_k[None]
 

time: 34.5 us -> 32 us (0.928)
  local copies, waits for them, and re-layouts: 3.09 us -> 1.31 us
  Pallas kernels: 28.8 us -> 28.2 us
    unnamed x2, local copies, waits for them, and re-layouts: 3.09 us -> 1.31 us
    pallas_call x1, Pallas kernels: 28.8 us -> 28.2 us  [shards(): pl.pallas_call(functools.partial(kernel, n, heads, group), out_shape=(jax...]
where the time goes in v3:
time: 32 us; the launch traced here: 31.8 us
  Pallas kernels  28.2 us (88%)
  between operations  2.33 us (7%)
  local copies, waits for them, and re-layouts  1.31 us (4%)
    pallas_call x1, Pallas kernels, shards(): pl.pallas_call(functools.partial(kernel, n, heads, group), out_shape=(jax...  28.2 us
    unnamed x2, local copies, waits for them, and re-layouts  1.31 us

profile of v3, /device:TPU:0, one launch (start us, length us, event | category | flops | bytes accessed | tf_op | source)
XLA Modules:
  0.0 31.8 jit_solution(4522692421138563657)
XLA Ops:
  0.6 28.2 %shard_map.76 = (f32[1,1]{1,0:T(1,128)}, f32[128,128]{1,0:T(8,128)S(1)}, f32[384,128]{1,0:T(8,128)S(1)}) custom-call(s32[4]{0:T(128)} %order_hbm.1, bf16[2048,128]{1,0:T(8,128)(2,1)} %bitcast.9, bf16[256,128]{1,0:T(8,128)(2,1)} %bitcast.11, bf16[128,128]{1,0:T(8,128)(2,1)} %bitcast.12, bf16[384,128]{1,0:T(8,128)(2,1)} %bitcast.10), custom_call_target="tpu_custom_call" | custom-call | tf_op jit(solution)/shard_map/pallas_call | solution.py:279
  28.8 0.6 %copy.11 = f32[1,128,128]{2,1,0:T(8,128)} copy(f32[1,128,128]{2,1,0:T(8,128)S(1)} %bitcast.8) | data formatting | bytes 131072
  29.4 0.7 %copy.12 = f32[1,384,128]{2,1,0:T(8,128)} copy(f32[1,384,128]{2,1,0:T(8,128)S(1)} %bitcast.7) | data formatting | bytes 393216

commit v4 on v3

--- a/solution.py
+++ b/solution.py
@@ -10,7 +10,6 @@
 
 BLOCK = 64
 MESH = pl.DeviceIdType.MESH
-HIGH = lax.Precision.HIGHEST
 F32 = jnp.float32
 BF16 = jnp.bfloat16
 MASKED = -1e30
@@ -18,6 +17,21 @@
 TN = (((0,), (0,)), ((), ()))
 LANES = 128
 STEP = 32
+
+
+def parts(x):
+    high = x.astype(BF16)
+    return high, (x - high.astype(F32)).astype(BF16)
+
+
+def product(x, y, dims=(((1,), (0,)), ((), ()))):
+    (xc,), (yc,) = dims[0]
+    xs = parts(x) if x.dtype == F32 else (x,)
+    ys = parts(y) if y.dtype == F32 else (y,)
+    pairs = [(i, j) for i in range(len(xs)) for j in range(len(ys)) if i + j < 2]
+    left = jnp.concatenate([xs[i] for i, _ in pairs], axis=xc)
+    right = jnp.concatenate([ys[j] for _, j in pairs], axis=yc)
+    return lax.dot_general(left, right, dims, preferred_element_type=F32)
 
 
 def kernel(
@@ -29,12 +43,12 @@
 ):
     tok, width = k_hbm.shape
     local = tok // BLOCK
-    extra = kbuf.shape[1] - tok
+    width_q = local * group
+    extra = kbuf.shape[1] - tok - width_q
     blocks = n * local
     span = BLOCK * group
     far = n // 2
-    scale = width ** (-0.5)
-    k2 = scale * math.log2(math.e)
+    k2 = width ** (-0.5) * math.log2(math.e)
     me = lax.axis_index("seq")
     head = lax.axis_index("head")
     a, r = me // 2, me % 2
@@ -71,6 +85,15 @@
         for m, piece in enumerate(pieces):
             tail = jnp.where(row == 4 * i + m, piece, tail)
     kbuf[me, pl.ds(tok, extra), :] = tail.astype(BF16)
+    fetch[2].wait()
+    qpool = [
+        jnp.sum(
+            q_ref[pl.ds(b * span, span), :].astype(F32).reshape(BLOCK, group, width), axis=0
+        )
+        for b in range(local)
+    ]
+    qp = (jnp.concatenate(qpool, axis=0) * (1.0 / BLOCK)).astype(BF16)
+    kbuf[me, pl.ds(tok + extra, width_q), :] = qp
     pl.semaphore_wait(barrier, n - 1 + heads - 1)
 
     def key_copy(slot, send, to):
@@ -87,17 +110,12 @@
     for copy in sends:
         copy.start()
 
-    fetch[2].wait()
-    qpool = []
     for b in range(local):
-        data = q_ref[pl.ds(b * span, span), :]
-        qt[:, pl.ds(b * span, span)] = data.T
-        qpool.append(jnp.sum(data.astype(F32).reshape(BLOCK, group, width), axis=0))
-    qpool.append(jnp.zeros((LANES - local * group, width), F32))
-    qp = (jnp.concatenate(qpool, axis=0) * (1.0 / BLOCK)).astype(BF16)
+        qt[:, pl.ds(b * span, span)] = q_ref[pl.ds(b * span, span), :].T
     fetch[3].wait()
     fetch[4].wait()
     qproj = jnp.dot(qp, gq_ref[...], preferred_element_type=F32)
+    qproj = jnp.concatenate([qproj, jnp.zeros((LANES - width_q, qproj.shape[1]), F32)], axis=0)
     rmax[...] = jnp.full_like(rmax, MASKED)
     rsum[...] = jnp.zeros_like(rsum)
 
@@ -198,12 +216,12 @@
         here_lanes = lane // group == b
         pooled = jnp.where(here_lanes, best, pooled)
         mine = jnp.where(here_lanes, order_ref[b].astype(F32), mine)
-    valid = lane < local * group
+    valid = lane < width_q
     pooled = jnp.exp2(pooled)
     target = pooled / jnp.sum(pooled, axis=0, keepdims=True)
 
     gscale = gq_ref.shape[1] ** (-0.5)
-    logits = lax.dot_general(kproj, qproj, NT, precision=HIGH, preferred_element_type=F32) * gscale
+    logits = product(kproj, qproj, NT) * gscale
     logits = jnp.where(ords[:, 0, :] > mine, MASKED, logits)
     shifted = logits - jnp.max(logits, axis=0, keepdims=True)
     weight = jnp.exp(shifted)
@@ -214,10 +232,16 @@
     terms = jnp.where((target > 0) & valid, target * (safe - logp), 0.0) * (1.0 / count)
     rowtot = jnp.sum(target, axis=0, keepdims=True)
     dlogit = jnp.where(valid, (weight / norm * rowtot - target) * (gscale / count), 0.0)
-    mbuf[me, pl.ds(0, blocks), :] = jnp.dot(
-        dlogit, qp.astype(F32), precision=HIGH, preferred_element_type=F32
-    )
-    mbuf[me, pl.ds(blocks, 8), :] = jnp.sum(terms.reshape(blocks // 8, 8, LANES), axis=0)
+    share = LANES // width_q
+    packed = blocks // share
+    for v in range(packed // 8):
+        rolled = [
+            pltpu.roll(dlogit[(v * share + g) * 8:(v * share + g + 1) * 8], g * width_q, 1) if g else
+            dlogit[v * share * 8:(v * share + 1) * 8]
+            for g in range(share)
+        ]
+        mbuf[me, pl.ds(v * 8, 8), :] = functools.reduce(jnp.add, rolled)
+    mbuf[me, pl.ds(packed, 8), :] = jnp.sum(terms.reshape(blocks // 8, 8, LANES), axis=0)
 
     def sum_copy(slot, k, to):
         return pltpu.make_async_remote_copy(
@@ -230,11 +254,7 @@
         copy.start()
     for k in range(1, n):
         sum_copy((me + k) % n, k, me).wait_recv()
-    total = mbuf[0]
-    for slot in range(1, n):
-        total = total + mbuf[slot]
-
-    lbuf[head] = total[blocks:]
+    lbuf[head] = jnp.sum(mbuf[:, packed:, :], axis=0)
 
     def loss_copy(slot, k, to):
         return pltpu.make_async_remote_copy(
@@ -245,12 +265,26 @@
     losses = [loss_copy(head, k, (head + k) % heads) for k in range(1, heads)]
     for copy in losses:
         copy.start()
-    grad = total[:blocks]
-    dq_ref[...] = lax.dot_general(grad, kproj, TN, precision=HIGH, preferred_element_type=F32)
-    dkproj = jnp.dot(grad, gq_ref[...].astype(F32), precision=HIGH, preferred_element_type=F32)
-    dk_ref[...] = lax.dot_general(
-        kpool.astype(F32), dkproj, TN, precision=HIGH, preferred_element_type=F32
+    tiles_of = []
+    for t in range(blocks // 8):
+        chunks = []
+        for first in range(0, n, share):
+            chunk = jnp.zeros((8, LANES), F32)
+            for g in range(share):
+                piece = mbuf[first + g, pl.ds(t // share * 8, 8), :]
+                if g != t % share:
+                    piece = pltpu.roll(piece, (g - t % share) % share * width_q, 1)
+                chunk = jnp.where(lane // width_q == g, piece, chunk)
+            chunks.append(chunk)
+        tiles_of.append(jnp.concatenate(chunks, axis=1))
+    dlogits = jnp.concatenate(tiles_of, axis=0)
+    queries = kbuf[:, tok + extra:, :].reshape(n * width_q, width)
+    high, low = parts(dlogits)
+    grad = jnp.dot(high, queries, preferred_element_type=F32) + jnp.dot(
+        low, queries, preferred_element_type=F32
     )
+    dq_ref[...] = product(grad, kproj, TN)
+    dk_ref[...] = product(kpool, product(grad, gq_ref[...]), TN)
     for k in range(1, heads):
         loss_copy((head + k) % heads, k, head).wait_recv()
     loss = lbuf[0]
@@ -286,7 +320,7 @@
             in_specs=[hbm] * 5,
             out_specs=(smem, vmem, vmem),
             scratch_shapes=[
-                pltpu.VMEM((n, tok + extra, width), BF16),
+                pltpu.VMEM((n, tok + extra + local * group, width), BF16),
                 pltpu.VMEM((blocks, 8, tok * group), F32),
                 pltpu.VMEM((8, tok * group), F32),
                 pltpu.VMEM((8, tok * group), F32),
@@ -295,7 +329,7 @@
                 block_rows,
                 block_rows,
                 pltpu.VMEM((local, blocks, 8, width), F32),
-                pltpu.VMEM((n, blocks + 8, width), F32),
+                pltpu.VMEM((n, blocks * local * group // LANES + 8, width), F32),
                 pltpu.VMEM((heads, 8, width), F32),
                 pltpu.SMEM((local,), jnp.int32),
                 pltpu.VMEM((tok * group, width), BF16),

time: 32 us -> 32.2 us (level)
  no operation moved by 1% of the time
where the time goes in v4:
time: 32.2 us; the launch traced here: 32 us
  Pallas kernels  28.4 us (88%)
  between operations  2.33 us (7%)
  local copies, waits for them, and re-layouts  1.31 us (4%)
    pallas_call x1, Pallas kernels, shards(): pl.pallas_call(functools.partial(kernel, n, heads, group), out_shape=(jax...  28.4 us
    unnamed x2, local copies, waits for them, and re-layouts  1.31 us

profile of v4, /device:TPU:0, one launch (start us, length us, event | category | flops | bytes accessed | tf_op | source)
XLA Modules:
  0.0 32.0 jit_solution(10651008748856309348)
XLA Ops:
  0.6 28.4 %shard_map.76 = (f32[1,1]{1,0:T(1,128)}, f32[128,128]{1,0:T(8,128)S(1)}, f32[384,128]{1,0:T(8,128)S(1)}) custom-call(s32[4]{0:T(128)} %order_hbm.1, bf16[2048,128]{1,0:T(8,128)(2,1)} %bitcast.9, bf16[256,128]{1,0:T(8,128)(2,1)} %bitcast.11, bf16[128,128]{1,0:T(8,128)(2,1)} %bitcast.12, bf16[384,128]{1,0:T(8,128)(2,1)} %bitcast.10), custom_call_target="tpu_custom_call" | custom-call | tf_op jit(solution)/shard_map/pallas_call | solution.py:313
  29.0 0.6 %copy.11 = f32[1,128,128]{2,1,0:T(8,128)} copy(f32[1,128,128]{2,1,0:T(8,128)S(1)} %bitcast.8) | data formatting | bytes 131072
  29.7 0.7 %copy.12 = f32[1,384,128]{2,1,0:T(8,128)} copy(f32[1,384,128]{2,1,0:T(8,128)S(1)} %bitcast.7) | data formatting | bytes 393216

commit v5 on v4

--- a/solution.py
+++ b/solution.py
@@ -39,7 +39,7 @@
     loss_ref, dq_ref, dk_ref,
     kbuf, bmax, rmax, rsum, ords, kmax, kmin, kmean, top, mbuf, lbuf,
     order_ref, q_ref, qt, gq_ref, gk_ref,
-    ksend, krecv, fsend, msend, mrecv, lsend, lrecv, held,
+    csend, dsend, krecv, fsend, msend, mrecv, lsend, lrecv, held,
 ):
     tok, width = k_hbm.shape
     local = tok // BLOCK
@@ -102,13 +102,27 @@
             device_id={"seq": to}, device_id_type=MESH,
         )
 
-    sends = []
-    for k in range(1, far):
-        to = (a + k) % far * 2 + r
-        sends.append(key_copy(me, ksend.at[k], to))
-    sends.insert(1, key_copy(me, ksend.at[0], partner))
-    for copy in sends:
-        copy.start()
+    def onward(source, side):
+        goes = (a + side >= 0) & (a + side < far) & ((a - source) * side >= 0)
+        slot = source * 2 + r
+        sem = csend.at[slot] if side > 0 else dsend.at[slot]
+        return goes, key_copy(slot, sem, (a + side) * 2 + r)
+
+    def across(source):
+        slot = source * 2 + r
+        return key_copy(slot, fsend.at[slot], partner)
+
+    for side in (1, -1):
+        goes, copy = onward(a, side)
+        pl.when(goes)(copy.start)
+    across(a).start()
+
+    short = jnp.minimum(a, far - 1 - a)
+    longer = jnp.where(a < far - 1 - a, 1, -1)
+
+    def source_of(i):
+        near = jnp.where(i % 2 == 1, a - (i + 1) // 2, a + (i + 1) // 2)
+        return jnp.where(i <= 2 * short, near, a + longer * (i - short))
 
     for b in range(local):
         qt[:, pl.ds(b * span, span)] = q_ref[pl.ds(b * span, span), :].T
@@ -126,17 +140,20 @@
     )
 
     def wait_keys(slot):
-        key_copy(slot, ksend.at[0], partner).wait_recv()
+        key_copy(slot, fsend.at[slot], partner).wait_recv()
 
     def shard(j, _):
-        back = j // 2
-        slot = (a - back + far) % far * 2 + (r + j) % 2
-
-        @pl.when((j % 2 == 1) & (back + 1 < far))
-        def _():
-            direct = (a - back - 1 + far) % far * 2 + r
-            wait_keys(direct)
-            key_copy(direct, fsend.at[back + 1], partner).start()
+        slot = source_of(j // 2) * 2 + (r + j) % 2
+        step = (j + 1) // 2
+        for side in (1, -1):
+            source = a - side * step
+
+            @pl.when((j % 2 == 1) & (source >= 0) & (source < far))
+            def _():
+                wait_keys(source * 2 + r)
+                across(source).start()
+                goes, copy = onward(source, side)
+                pl.when(goes)(copy.start)
 
         @pl.when(j % 2 == 1)
         def _():
@@ -178,10 +195,6 @@
         return 0
 
     lax.fori_loop(0, n, shard, 0)
-    forwards = [
-        key_copy((a - k + far) % far * 2 + r, fsend.at[k], partner) for k in range(1, far)
-    ]
-
     kpool = jnp.concatenate([ref[:, 0, :] for ref in (kmax, kmin, kmean)], axis=1).astype(BF16)
     kproj = jnp.dot(kpool, gk_ref[...], preferred_element_type=F32)
 
@@ -291,8 +304,17 @@
     for slot in range(1, heads):
         loss = loss + lbuf[slot]
     loss_ref[0, 0] = jnp.sum(loss)
-    for copy in sends + forwards + shares + losses:
+    for copy in shares + losses:
         copy.wait_send()
+
+    def sent(source, _):
+        across(source).wait_send()
+        for side in (1, -1):
+            goes, copy = onward(source, side)
+            pl.when(goes)(copy.wait_send)
+        return 0
+
+    lax.fori_loop(0, far, sent, 0)
 
 
 def solution(mesh):
@@ -336,7 +358,7 @@
                 pltpu.VMEM((width, tok * group), BF16),
                 pltpu.VMEM((width, dim), BF16),
                 pltpu.VMEM((pooled, dim), BF16),
-                dma((n,)), dma((n,)), dma((n,)), dma((n,)), dma((n,)), dma((heads,)), dma((heads,)), dma((5,)),
+                dma((n,)), dma((n,)), dma((n,)), dma((n,)), dma((n,)), dma((n,)), dma((heads,)), dma((heads,)), dma((5,)),
             ],
             compiler_params=pltpu.CompilerParams(
                 collective_id=0, has_side_effects=True, vmem_limit_bytes=48 << 20

time: 32.2 us -> 33.1 us (1.028)
  Pallas kernels: 28.4 us -> 29.3 us
    pallas_call x1, Pallas kernels: 28.4 us -> 29.3 us  [shards(): pl.pallas_call(functools.partial(kernel, n, heads, group), out_shape=(jax...]
where the time goes in v5:
time: 33.1 us; the launch traced here: 32.9 us
  Pallas kernels  29.3 us (89%)
  between operations  2.33 us (7%)
  local copies, waits for them, and re-layouts  1.31 us (4%)
    pallas_call x1, Pallas kernels, shards(): pl.pallas_call(functools.partial(kernel, n, heads, group), out_shape=(jax...  29.3 us
    unnamed x2, local copies, waits for them, and re-layouts  1.31 us

profile of v5, /device:TPU:0, one launch (start us, length us, event | category | flops | bytes accessed | tf_op | source)
XLA Modules:
  0.0 32.9 jit_solution(2802950424478506500)
XLA Ops:
  0.6 29.3 %shard_map.76 = (f32[1,1]{1,0:T(1,128)}, f32[128,128]{1,0:T(8,128)S(1)}, f32[384,128]{1,0:T(8,128)S(1)}) custom-call(s32[4]{0:T(128)} %order_hbm.1, bf16[2048,128]{1,0:T(8,128)(2,1)} %bitcast.9, bf16[256,128]{1,0:T(8,128)(2,1)} %bitcast.11, bf16[128,128]{1,0:T(8,128)(2,1)} %bitcast.12, bf16[384,128]{1,0:T(8,128)(2,1)} %bitcast.10), custom_call_target="tpu_custom_call" | custom-call | tf_op jit(solution)/shard_map/pallas_call | solution.py:335
  29.9 0.6 %copy.11 = f32[1,128,128]{2,1,0:T(8,128)} copy(f32[1,128,128]{2,1,0:T(8,128)S(1)} %bitcast.8) | data formatting | bytes 131072
  30.6 0.7 %copy.12 = f32[1,384,128]{2,1,0:T(8,128)} copy(f32[1,384,128]{2,1,0:T(8,128)S(1)} %bitcast.7) | data formatting | bytes 393216

commit v6 on v4

--- a/solution.py
+++ b/solution.py
@@ -34,10 +34,27 @@
     return lax.dot_general(left, right, dims, preferred_element_type=F32)
 
 
+def row_maxima(rows):
+    at = lax.broadcasted_iota(jnp.int32, rows[0].shape, 0)
+    shift = 4
+    while shift:
+        low = at % (2 * shift) < shift
+        merged = []
+        for x, y in zip(rows[:shift], rows[shift:]):
+            keep, move = jnp.where(low, x, y), jnp.where(low, y, x)
+            moved = pltpu.roll(move, shift, 0)
+            if shift < 4:
+                moved = jnp.where(low, pltpu.roll(move, 8 - shift, 0), moved)
+            merged.append(jnp.maximum(keep, moved))
+        rows = merged
+        shift //= 2
+    return rows[0]
+
+
 def kernel(
     n, heads, group, order_hbm, q_hbm, k_hbm, gq_hbm, gk_hbm,
     loss_ref, dq_ref, dk_ref,
-    kbuf, bmax, rmax, rsum, ords, kmax, kmin, kmean, top, mbuf, lbuf,
+    kbuf, bmax, rmax, rsum, ords, kmax, kmin, kmean, top, scores, mbuf, lbuf,
     order_ref, q_ref, qt, gq_ref, gk_ref,
     ksend, krecv, fsend, msend, mrecv, lsend, lrecv, held,
 ):
@@ -121,8 +138,8 @@
 
     half = span // 2
 
-    ahead = lax.broadcasted_iota(jnp.int32, (BLOCK, half), 0) - (
-        lax.broadcasted_iota(jnp.int32, (BLOCK, half), 1) // group
+    ahead = lax.broadcasted_iota(jnp.int32, (BLOCK, LANES), 0) - (
+        lax.broadcasted_iota(jnp.int32, (BLOCK, LANES), 1) // group
     )
 
     def wait_keys(slot):
@@ -149,23 +166,33 @@
                 ref[at] = jnp.broadcast_to(tail[4 * i + m:4 * i + m + 1], (8, width))
         unmasked = jnp.where(j == 0, 0, 2 * BLOCK)
 
-        for b in range(local):
+        spread = [jnp.broadcast_to(tail[4 * i:4 * i + 1], (8, width)) for i in range(local)]
+
+        def multiply(t):
+            scores[t % 2] = jnp.dot(
+                kbuf[slot, pl.ds(0, tok), :], qt[:, pl.ds(t * half, half)],
+                preferred_element_type=F32,
+            )
+
+        count = 2 * local
+        multiply(0)
+        for t in range(count):
+            if t + 1 < count:
+                multiply(t + 1)
+            b, part = t // 2, t % 2
             here = order_ref[b].astype(F32)
-            for part in range(2):
-                cols = pl.ds(b * span + part * half, half)
-                scores = jnp.dot(
-                    kbuf[slot, pl.ds(0, tok), :], qt[:, cols], preferred_element_type=F32
-                )
+            for lanes in range(0, half, LANES):
+                cols = pl.ds(t * half + lanes, LANES)
                 highs, sums = [], []
                 for i in range(local):
-                    s = scores[i * BLOCK:(i + 1) * BLOCK]
+                    s = scores[t % 2, pl.ds(i * BLOCK, BLOCK), pl.ds(lanes, LANES)]
                     if b == i:
-                        s = jnp.where(ahead > unmasked + part * (BLOCK // 2), MASKED / k2, s)
-                    s = s.reshape(BLOCK // 8, 8, half)
+                        limit = unmasked + (part * half + lanes) // group
+                        s = jnp.where(ahead > limit, MASKED / k2, s)
+                    s = s.reshape(BLOCK // 8, 8, LANES)
                     high = jnp.max(s, axis=0)
                     sums.append(jnp.sum(jnp.exp2((s - high) * k2), axis=0))
-                    later = jnp.broadcast_to(tail[4 * i:4 * i + 1, :1], (8, half)) > here
-                    high = jnp.where(later, MASKED, high * k2)
+                    high = jnp.where(spread[i] > here, MASKED, high * k2)
                     bmax[slot * local + i, :, cols] = high
                     highs.append(high)
                 old = rmax[:, cols]
@@ -199,16 +226,20 @@
             lse.append(high + jnp.log2(total))
 
         def tops(step, _):
-            for j in range(STEP):
-                c = step * STEP + j
-                best = [
-                    bmax[c, :, pl.ds(b * span + t * LANES, LANES)] - lse[t] for t in range(tiles)
-                ]
-                top[b, c] = functools.reduce(jnp.maximum, best)
+            for eight in range(STEP // 8):
+                first = pl.multiple_of(step * STEP + eight * 8, 8)
+                rows = []
+                for j in range(8):
+                    best = [
+                        bmax[first + j, :, pl.ds(b * span + t * LANES, LANES)] - lse[t]
+                        for t in range(tiles)
+                    ]
+                    rows.append(functools.reduce(jnp.maximum, best))
+                top[b, pl.ds(first, 8), :] = row_maxima(rows)
             return 0
 
         lax.fori_loop(0, blocks // STEP, tops, 0)
-        best = jnp.max(top[b], axis=1)
+        best = top[b]
         shift = group
         while shift < LANES:
             best = jnp.maximum(best, pltpu.roll(best, shift, 1))
@@ -328,7 +359,8 @@
                 block_rows,
                 block_rows,
                 block_rows,
-                pltpu.VMEM((local, blocks, 8, width), F32),
+                pltpu.VMEM((local, blocks, width), F32),
+                pltpu.VMEM((2, tok, BLOCK * group // 2), F32),
                 pltpu.VMEM((n, blocks * local * group // LANES + 8, width), F32),
                 pltpu.VMEM((heads, 8, width), F32),
                 pltpu.SMEM((local,), jnp.int32),

time: 32.2 us -> 32.2 us (level)
  no operation moved by 1% of the time
where the time goes in v6:
time: 32.2 us; the launch traced here: 32.1 us
  Pallas kernels  28.4 us (88%)
  between operations  2.33 us (7%)
  local copies, waits for them, and re-layouts  1.31 us (4%)
    pallas_call x1, Pallas kernels, shards(): pl.pallas_call(functools.partial(kernel, n, heads, group), out_shape=(jax...  28.4 us
    unnamed x2, local copies, waits for them, and re-layouts  1.31 us

profile of v6, /device:TPU:0, one launch (start us, length us, event | category | flops | bytes accessed | tf_op | source)
XLA Modules:
  0.0 32.1 jit_solution(17169259509283526953)
XLA Ops:
  0.6 28.4 %shard_map.76 = (f32[1,1]{1,0:T(1,128)}, f32[128,128]{1,0:T(8,128)S(1)}, f32[384,128]{1,0:T(8,128)S(1)}) custom-call(s32[4]{0:T(128)} %order_hbm.1, bf16[2048,128]{1,0:T(8,128)(2,1)} %bitcast.9, bf16[256,128]{1,0:T(8,128)(2,1)} %bitcast.11, bf16[128,128]{1,0:T(8,128)(2,1)} %bitcast.12, bf16[384,128]{1,0:T(8,128)(2,1)} %bitcast.10), custom_call_target="tpu_custom_call" | custom-call | tf_op jit(solution)/shard_map/pallas_call | solution.py:344
  29.1 0.6 %copy.11 = f32[1,128,128]{2,1,0:T(8,128)} copy(f32[1,128,128]{2,1,0:T(8,128)S(1)} %bitcast.8) | data formatting | bytes 131072
  29.7 0.7 %copy.12 = f32[1,384,128]{2,1,0:T(8,128)} copy(f32[1,384,128]{2,1,0:T(8,128)S(1)} %bitcast.7) | data formatting | bytes 393216

commit v7 on v6

--- a/solution.py
+++ b/solution.py
@@ -191,7 +191,12 @@
                         s = jnp.where(ahead > limit, MASKED / k2, s)
                     s = s.reshape(BLOCK // 8, 8, LANES)
                     high = jnp.max(s, axis=0)
-                    sums.append(jnp.sum(jnp.exp2((s - high) * k2), axis=0))
+                    power = jnp.exp2(((s - high) * k2).astype(BF16).reshape(BLOCK, LANES))
+                    half_sums = [power[w:w + 16] for w in range(0, BLOCK, 16)]
+                    while len(half_sums) > 1:
+                        half_sums = [u + v for u, v in zip(half_sums[::2], half_sums[1::2])]
+                    pair_sum = half_sums[0].astype(F32)
+                    sums.append(pair_sum[:8] + pair_sum[8:])
                     high = jnp.where(spread[i] > here, MASKED, high * k2)
                     bmax[slot * local + i, :, cols] = high
                     highs.append(high)

time: 32.2 us -> 32.9 us (1.022)
  Pallas kernels: 28.4 us -> 29.1 us
    pallas_call x1, Pallas kernels: 28.4 us -> 29.1 us  [shards(): pl.pallas_call(functools.partial(kernel, n, heads, group), out_shape=(jax...]
where the time goes in v7:
time: 32.9 us; the launch traced here: 32.8 us
  Pallas kernels  29.1 us (88%)
  between operations  2.33 us (7%)
  local copies, waits for them, and re-layouts  1.31 us (4%)
    pallas_call x1, Pallas kernels, shards(): pl.pallas_call(functools.partial(kernel, n, heads, group), out_shape=(jax...  29.1 us
    unnamed x2, local copies, waits for them, and re-layouts  1.31 us

profile of v7, /device:TPU:0, one launch (start us, length us, event | category | flops | bytes accessed | tf_op | source)
XLA Modules:
  0.0 32.8 jit_solution(15874929203483987883)
XLA Ops:
  0.6 29.1 %shard_map.76 = (f32[1,1]{1,0:T(1,128)}, f32[128,128]{1,0:T(8,128)S(1)}, f32[384,128]{1,0:T(8,128)S(1)}) custom-call(s32[4]{0:T(128)} %order_hbm.1, bf16[2048,128]{1,0:T(8,128)(2,1)} %bitcast.9, bf16[256,128]{1,0:T(8,128)(2,1)} %bitcast.11, bf16[128,128]{1,0:T(8,128)(2,1)} %bitcast.12, bf16[384,128]{1,0:T(8,128)(2,1)} %bitcast.10), custom_call_target="tpu_custom_call" | custom-call | tf_op jit(solution)/shard_map/pallas_call | solution.py:349
  29.8 0.6 %copy.11 = f32[1,128,128]{2,1,0:T(8,128)} copy(f32[1,128,128]{2,1,0:T(8,128)S(1)} %bitcast.8) | data formatting | bytes 131072
  30.4 0.7 %copy.12 = f32[1,384,128]{2,1,0:T(8,128)} copy(f32[1,384,128]{2,1,0:T(8,128)S(1)} %bitcast.7) | data formatting | bytes 393216

commit v8 on v6

--- a/solution.py
+++ b/solution.py
@@ -61,7 +61,8 @@
     tok, width = k_hbm.shape
     local = tok // BLOCK
     width_q = local * group
-    extra = kbuf.shape[1] - tok - width_q
+    extra = kbuf.shape[1] // 2 - tok - width_q
+    side = extra + width_q
     blocks = n * local
     span = BLOCK * group
     far = n // 2
@@ -69,6 +70,8 @@
     me = lax.axis_index("seq")
     head = lax.axis_index("head")
     a, r = me // 2, me % 2
+    keys_at = pl.multiple_of(side + r * tok, 16)
+    side_at = pl.multiple_of(r * (side + 2 * tok), 16)
     partner = a * 2 + (r + 1) % 2
 
     barrier = pltpu.get_barrier_semaphore()
@@ -78,7 +81,7 @@
         pl.semaphore_signal(barrier, inc=1, device_id={"head": (head + k) % heads}, device_id_type=MESH)
 
     fetch = [
-        pltpu.make_async_copy(k_hbm, kbuf.at[me, pl.ds(0, tok), :], held.at[0]),
+        pltpu.make_async_copy(k_hbm, kbuf.at[a, pl.ds(keys_at, tok), :], held.at[0]),
         pltpu.make_async_copy(order_hbm, order_ref, held.at[1]),
         pltpu.make_async_copy(q_hbm, q_ref, held.at[2]),
         pltpu.make_async_copy(gq_hbm, gq_ref, held.at[3]),
@@ -92,7 +95,7 @@
     row = lax.broadcasted_iota(jnp.int32, (extra, width), 0)
     tail = jnp.zeros((extra, width), F32)
     for i in range(local):
-        part = kbuf[me, pl.ds(i * BLOCK, BLOCK), :].astype(F32).reshape(BLOCK // 8, 8, width)
+        part = kbuf[a, pl.ds(pl.multiple_of(keys_at + i * BLOCK, 16), BLOCK), :].astype(F32).reshape(BLOCK // 8, 8, width)
         pieces = (
             order_ref[i].astype(F32),
             jnp.max(jnp.max(part, axis=0), axis=0, keepdims=True),
@@ -101,7 +104,7 @@
         )
         for m, piece in enumerate(pieces):
             tail = jnp.where(row == 4 * i + m, piece, tail)
-    kbuf[me, pl.ds(tok, extra), :] = tail.astype(BF16)
+    kbuf[a, pl.ds(side_at, extra), :] = tail.astype(BF16)
     fetch[2].wait()
     qpool = [
         jnp.sum(
@@ -110,12 +113,14 @@
         for b in range(local)
     ]
     qp = (jnp.concatenate(qpool, axis=0) * (1.0 / BLOCK)).astype(BF16)
-    kbuf[me, pl.ds(tok + extra, width_q), :] = qp
+    kbuf[a, pl.ds(pl.multiple_of(side_at + extra, 16), width_q), :] = qp
     pl.semaphore_wait(barrier, n - 1 + heads - 1)
 
     def key_copy(slot, send, to):
+        rows = pl.ds(pl.multiple_of(slot % 2 * (side + tok), 16), side + tok)
+        at = slot // 2
         return pltpu.make_async_remote_copy(
-            src_ref=kbuf.at[slot], dst_ref=kbuf.at[slot], send_sem=send, recv_sem=krecv.at[slot],
+            src_ref=kbuf.at[at, rows], dst_ref=kbuf.at[at, rows], send_sem=send, recv_sem=krecv.at[slot],
             device_id={"seq": to}, device_id_type=MESH,
         )
 
@@ -145,38 +150,34 @@
     def wait_keys(slot):
         key_copy(slot, ksend.at[0], partner).wait_recv()
 
-    def shard(j, _):
-        back = j // 2
-        slot = (a - back + far) % far * 2 + (r + j) % 2
-
-        @pl.when((j % 2 == 1) & (back + 1 < far))
-        def _():
-            direct = (a - back - 1 + far) % far * 2 + r
-            wait_keys(direct)
-            key_copy(direct, fsend.at[back + 1], partner).start()
-
-        @pl.when(j % 2 == 1)
-        def _():
-            wait_keys(slot)
-
-        tail = kbuf[slot, pl.ds(tok, extra), :].astype(F32)
-        for i in range(local):
-            at = slot * local + i
-            for m, ref in enumerate((ords, kmax, kmin, kmean)):
-                ref[at] = jnp.broadcast_to(tail[4 * i + m:4 * i + m + 1], (8, width))
-        unmasked = jnp.where(j == 0, 0, 2 * BLOCK)
-
-        spread = [jnp.broadcast_to(tail[4 * i:4 * i + 1], (8, width)) for i in range(local)]
+    def shards(k, _):
+        line = (a - k + far) % far
+        wait_keys(line * 2 + (r + 1) % 2)
+        spread = []
+        for p in range(2):
+            tail = kbuf[line, pl.ds(p * (side + 2 * tok), extra), :].astype(F32)
+            for i in range(local):
+                at = line * 2 * local + p * local + i
+                for m, ref in enumerate((ords, kmax, kmin, kmean)):
+                    ref[at] = jnp.broadcast_to(tail[4 * i + m:4 * i + m + 1], (8, width))
+                spread.append(jnp.broadcast_to(tail[4 * i:4 * i + 1], (8, width)))
+        unmasked = [jnp.where((k == 0) & (r == p), 0, 2 * BLOCK) for p in range(2)]
 
         def multiply(t):
             scores[t % 2] = jnp.dot(
-                kbuf[slot, pl.ds(0, tok), :], qt[:, pl.ds(t * half, half)],
+                kbuf[line, pl.ds(side, 2 * tok), :], qt[:, pl.ds(t * half, half)],
                 preferred_element_type=F32,
             )
 
         count = 2 * local
         multiply(0)
         for t in range(count):
+            if t == count // 2:
+                @pl.when(k + 1 < far)
+                def _():
+                    direct = (a - k - 1 + far) % far * 2 + r
+                    wait_keys(direct)
+                    key_copy(direct, fsend.at[k + 1], partner).start()
             if t + 1 < count:
                 multiply(t + 1)
             b, part = t // 2, t % 2
@@ -184,16 +185,16 @@
             for lanes in range(0, half, LANES):
                 cols = pl.ds(t * half + lanes, LANES)
                 highs, sums = [], []
-                for i in range(local):
+                for i in range(2 * local):
                     s = scores[t % 2, pl.ds(i * BLOCK, BLOCK), pl.ds(lanes, LANES)]
-                    if b == i:
-                        limit = unmasked + (part * half + lanes) // group
+                    if b == i % local:
+                        limit = unmasked[i // local] + (part * half + lanes) // group
                         s = jnp.where(ahead > limit, MASKED / k2, s)
                     s = s.reshape(BLOCK // 8, 8, LANES)
                     high = jnp.max(s, axis=0)
                     sums.append(jnp.sum(jnp.exp2((s - high) * k2), axis=0))
                     high = jnp.where(spread[i] > here, MASKED, high * k2)
-                    bmax[slot * local + i, :, cols] = high
+                    bmax[line * 2 * local + i, :, cols] = high
                     highs.append(high)
                 old = rmax[:, cols]
                 new = functools.reduce(jnp.maximum, highs, old)
@@ -204,7 +205,7 @@
                 rsum[:, cols] = total
         return 0
 
-    lax.fori_loop(0, n, shard, 0)
+    lax.fori_loop(0, far, shards, 0)
     forwards = [
         key_copy((a - k + far) % far * 2 + r, fsend.at[k], partner) for k in range(1, far)
     ]
@@ -309,7 +310,13 @@
             chunks.append(chunk)
         tiles_of.append(jnp.concatenate(chunks, axis=1))
     dlogits = jnp.concatenate(tiles_of, axis=0)
-    queries = kbuf[:, tok + extra:, :].reshape(n * width_q, width)
+    queries = jnp.concatenate(
+        [
+            kbuf[slot // 2, pl.ds(slot % 2 * (side + 2 * tok) + extra, width_q), :]
+            for slot in range(n)
+        ],
+        axis=0,
+    )
     high, low = parts(dlogits)
     grad = jnp.dot(high, queries, preferred_element_type=F32) + jnp.dot(
         low, queries, preferred_element_type=F32
@@ -351,7 +358,7 @@
             in_specs=[hbm] * 5,
             out_specs=(smem, vmem, vmem),
             scratch_shapes=[
-                pltpu.VMEM((n, tok + extra + local * group, width), BF16),
+                pltpu.VMEM((n // 2, 2 * (tok + extra + local * group), width), BF16),
                 pltpu.VMEM((blocks, 8, tok * group), F32),
                 pltpu.VMEM((8, tok * group), F32),
                 pltpu.VMEM((8, tok * group), F32),
@@ -360,7 +367,7 @@
                 block_rows,
                 block_rows,
                 pltpu.VMEM((local, blocks, width), F32),
-                pltpu.VMEM((2, tok, BLOCK * group // 2), F32),
+                pltpu.VMEM((2, 2 * tok, BLOCK * group // 2), F32),
                 pltpu.VMEM((n, blocks * local * group // LANES + 8, width), F32),
                 pltpu.VMEM((heads, 8, width), F32),
                 pltpu.SMEM((local,), jnp.int32),

time: 32.2 us -> 36.9 us (1.15)
  Pallas kernels: 28.4 us -> 33.1 us
    pallas_call x1, Pallas kernels: 28.4 us -> 33.1 us  [shards(): pl.pallas_call(functools.partial(kernel, n, heads, group), out_shape=(jax...]
where the time goes in v8:
time: 36.9 us; the launch traced here: 36.7 us
  Pallas kernels  33.1 us (90%)
  between operations  2.33 us (6%)
  local copies, waits for them, and re-layouts  1.31 us (4%)
    pallas_call x1, Pallas kernels, shards(): pl.pallas_call(functools.partial(kernel, n, heads, group), out_shape=(jax...  33.1 us
    unnamed x2, local copies, waits for them, and re-layouts  1.31 us

profile of v8, /device:TPU:0, one launch (start us, length us, event | category | flops | bytes accessed | tf_op | source)
XLA Modules:
  0.0 36.7 jit_solution(12693366162962859981)
XLA Ops:
  0.6 33.1 %shard_map.76 = (f32[1,1]{1,0:T(1,128)}, f32[128,128]{1,0:T(8,128)S(1)}, f32[384,128]{1,0:T(8,128)S(1)}) custom-call(s32[4]{0:T(128)} %order_hbm.1, bf16[2048,128]{1,0:T(8,128)(2,1)} %bitcast.9, bf16[256,128]{1,0:T(8,128)(2,1)} %bitcast.11, bf16[128,128]{1,0:T(8,128)(2,1)} %bitcast.12, bf16[384,128]{1,0:T(8,128)(2,1)} %bitcast.10), custom_call_target="tpu_custom_call" | custom-call | tf_op jit(solution)/shard_map/pallas_call | solution.py:351
  33.7 0.6 %copy.11 = f32[1,128,128]{2,1,0:T(8,128)} copy(f32[1,128,128]{2,1,0:T(8,128)S(1)} %bitcast.8) | data formatting | bytes 131072
  34.3 0.7 %copy.12 = f32[1,384,128]{2,1,0:T(8,128)} copy(f32[1,384,128]{2,1,0:T(8,128)S(1)} %bitcast.7) | data formatting | bytes 393216

commit v9 on v6

--- a/solution.py
+++ b/solution.py
@@ -56,7 +56,7 @@
     loss_ref, dq_ref, dk_ref,
     kbuf, bmax, rmax, rsum, ords, kmax, kmin, kmean, top, scores, mbuf, lbuf,
     order_ref, q_ref, qt, gq_ref, gk_ref,
-    ksend, krecv, fsend, msend, mrecv, lsend, lrecv, held,
+    ksend, krecv, msend, mrecv, lsend, lrecv, held,
 ):
     tok, width = k_hbm.shape
     local = tok // BLOCK
@@ -119,11 +119,9 @@
             device_id={"seq": to}, device_id_type=MESH,
         )
 
-    sends = []
-    for k in range(1, far):
-        to = (a + k) % far * 2 + r
-        sends.append(key_copy(me, ksend.at[k], to))
-    sends.insert(1, key_copy(me, ksend.at[0], partner))
+    sends = [
+        key_copy(me, ksend.at[j], (a + j // 2) % far * 2 + (r + j) % 2) for j in range(1, n)
+    ]
     for copy in sends:
         copy.start()
 
@@ -149,13 +147,7 @@
         back = j // 2
         slot = (a - back + far) % far * 2 + (r + j) % 2
 
-        @pl.when((j % 2 == 1) & (back + 1 < far))
-        def _():
-            direct = (a - back - 1 + far) % far * 2 + r
-            wait_keys(direct)
-            key_copy(direct, fsend.at[back + 1], partner).start()
-
-        @pl.when(j % 2 == 1)
+        @pl.when(j > 0)
         def _():
             wait_keys(slot)
 
@@ -205,10 +197,6 @@
         return 0
 
     lax.fori_loop(0, n, shard, 0)
-    forwards = [
-        key_copy((a - k + far) % far * 2 + r, fsend.at[k], partner) for k in range(1, far)
-    ]
-
     kpool = jnp.concatenate([ref[:, 0, :] for ref in (kmax, kmin, kmean)], axis=1).astype(BF16)
     kproj = jnp.dot(kpool, gk_ref[...], preferred_element_type=F32)
 
@@ -322,7 +310,7 @@
     for slot in range(1, heads):
         loss = loss + lbuf[slot]
     loss_ref[0, 0] = jnp.sum(loss)
-    for copy in sends + forwards + shares + losses:
+    for copy in sends + shares + losses:
         copy.wait_send()
 
 
@@ -368,7 +356,7 @@
                 pltpu.VMEM((width, tok * group), BF16),
                 pltpu.VMEM((width, dim), BF16),
                 pltpu.VMEM((pooled, dim), BF16),
-                dma((n,)), dma((n,)), dma((n,)), dma((n,)), dma((n,)), dma((heads,)), dma((heads,)), dma((5,)),
+                dma((n,)), dma((n,)), dma((n,)), dma((n,)), dma((heads,)), dma((heads,)), dma((5,)),
             ],
             compiler_params=pltpu.CompilerParams(
                 collective_id=0, has_side_effects=True, vmem_limit_bytes=48 << 20

time: 32.2 us -> 35.9 us (1.11)
  Pallas kernels: 28.4 us -> 32.1 us
    pallas_call x1, Pallas kernels: 28.4 us -> 32.1 us  [shards(): pl.pallas_call(functools.partial(kernel, n, heads, group), out_shape=(jax...]
where the time goes in v9:
time: 35.9 us; the launch traced here: 35.7 us
  Pallas kernels  32.1 us (89%)
  between operations  2.33 us (6%)
  local copies, waits for them, and re-layouts  1.31 us (4%)
    pallas_call x1, Pallas kernels, shards(): pl.pallas_call(functools.partial(kernel, n, heads, group), out_shape=(jax...  32.1 us
    unnamed x2, local copies, waits for them, and re-layouts  1.31 us

profile of v9, /device:TPU:0, one launch (start us, length us, event | category | flops | bytes accessed | tf_op | source)
XLA Modules:
  0.0 35.7 jit_solution(6742607414588832532)
XLA Ops:
  0.6 32.1 %shard_map.76 = (f32[1,1]{1,0:T(1,128)}, f32[128,128]{1,0:T(8,128)S(1)}, f32[384,128]{1,0:T(8,128)S(1)}) custom-call(s32[4]{0:T(128)} %order_hbm.1, bf16[2048,128]{1,0:T(8,128)(2,1)} %bitcast.9, bf16[256,128]{1,0:T(8,128)(2,1)} %bitcast.11, bf16[128,128]{1,0:T(8,128)(2,1)} %bitcast.12, bf16[384,128]{1,0:T(8,128)(2,1)} %bitcast.10), custom_call_target="tpu_custom_call" | custom-call | tf_op jit(solution)/shard_map/pallas_call | solution.py:332
  32.7 0.6 %copy.11 = f32[1,128,128]{2,1,0:T(8,128)} copy(f32[1,128,128]{2,1,0:T(8,128)S(1)} %bitcast.8) | data formatting | bytes 131072
  33.3 0.7 %copy.12 = f32[1,384,128]{2,1,0:T(8,128)} copy(f32[1,384,128]{2,1,0:T(8,128)S(1)} %bitcast.7) | data formatting | bytes 393216
